TPU v7x, 32 devices: a whole 2x2x4 slice. The times are simulated.
32 devices in a mesh: img: 4 (over y, x), grp: 8 (over z, core).
Axes of the slice: x: 2, y: 2, z: 4, core: 2. Of those that a mesh axis runs over, the one named last changes fastest.
Arguments:
- glob_x: bfloat16 [128, 14, 14, 512], P(('img', 'grp')), may hold values from -6 to 6
- loc_x: bfloat16 [384, 7, 7, 512], P(('img', 'grp')), may hold values from -6 to 6
- glob_cot: bfloat16 [128, 14, 14, 512], P(('img', 'grp')), may hold values from -6 to 6
- loc_cot: bfloat16 [384, 7, 7, 512], P(('img', 'grp')), may hold values from -6 to 6
- loc_extent: int32 [384, 2], P(('img', 'grp')), may hold values from 3 to 7
- glob_image: int32 [128], P('img'), may hold values from 0 to 15, as said below
- loc_image: int32 [384], P('img'), may hold values from 0 to 15, as said below
- s_kernels: bfloat16 [2, 9, 512], replicated, may hold values from -2 to 2
- s_gains: bfloat16 [2, 512], replicated, may hold values from 0.5 to 1.5
- s_shifts: bfloat16 [8, 512], replicated, may hold values from -1.5 to 1.5
- s_qkv: bfloat16 [512, 1536], replicated, may hold values from -0.25 to 0.25
- s_proj: bfloat16 [512, 512], replicated, may hold values from -1.5 to 1.5
- s_fc1: bfloat16 [512, 2048], replicated, may hold values from -0.25 to 0.25
- s_fc1_bias: bfloat16 [2048], replicated, may hold values from -1.5 to 1.5
- s_fc2: bfloat16 [2048, 512], replicated, may hold values from -0.125 to 0.125
- c_kernels: bfloat16 [2, 9, 512], replicated, may hold values from -2 to 2
- c_gains: bfloat16 [2, 512], replicated, may hold values from 0.5 to 1.5
- c_shifts: bfloat16 [9, 512], replicated, may hold values from -1.5 to 1.5
- c_qkv: bfloat16 [512, 1536], replicated, may hold values from -0.25 to 0.25
- c_proj: bfloat16 [512, 512], replicated, may hold values from -1 to 1
- c_fc1: bfloat16 [512, 2048], replicated, may hold values from -0.25 to 0.25
- c_fc1_bias: bfloat16 [2048], replicated, may hold values from -1.5 to 1.5
- c_fc2: bfloat16 [2048, 512], replicated, may hold values from -0.125 to 0.125
Outputs:
- glob_out: bfloat16 [128, 14, 14, 512], P(('img', 'grp'))
- loc_out: bfloat16 [384, 7, 7, 512], P(('img', 'grp'))
- glob_grad: float32 [128, 14, 14, 512], P(('img', 'grp'))
- loc_grad: float32 [384, 7, 7, 512], P(('img', 'grp'))
- s_kernels_grad: float32 [2, 9, 512], P(None, None, 'grp')
- s_gains_grad: float32 [2, 512], P(None, 'grp')
- s_shifts_grad: float32 [8, 512], P(None, 'grp')
- s_qkv_grad: float32 [512, 1536], P(None, 'grp')
- s_proj_grad: float32 [512, 512], P(None, 'grp')
- s_fc1_grad: float32 [512, 2048], P(None, 'grp')
- s_fc1_bias_grad: float32 [2048], P('grp')
- s_fc2_grad: float32 [2048, 512], P(None, 'grp')
- c_kernels_grad: float32 [2, 9, 512], P(None, None, 'grp')
- c_gains_grad: float32 [2, 512], P(None, 'grp')
- c_shifts_grad: float32 [9, 512], P(None, 'grp')
- c_qkv_grad: float32 [512, 1536], P(None, 'grp')
- c_proj_grad: float32 [512, 512], P(None, 'grp')
- c_fc1_grad: float32 [512, 2048], P(None, 'grp')
- c_fc1_bias_grad: float32 [2048], P('grp')
- c_fc2_grad: float32 [2048, 512], P(None, 'grp')
Inputs may be any that keep to these rules, and one draw needn't show every extreme that they name: `glob_image`: within each image row every one of its 16 images owns exactly 2 global crops. `loc_image`: within each image row every one of its 16 images owns exactly 6 local crops.
All inputs are finite; a program needn't handle non-finite values.
Results may differ from a plain program's by a relative error of at most 0.03.
Values may be sent and summed in bfloat16 or wider, within the bound.
No kernel may reach another device: no remote copies, remote signals or barrier semaphores. Data moves between devices by JAX's collectives and lax.ppermute only.
A program may use at most 320 MiB of HBM per device.

v0:
```python
import jax
import jax.numpy as jnp
from jax import lax
from jax.sharding import PartitionSpec as P

HEADS = 16
HEAD_DIM = 32
WIN = 7


PRECISE = lax.Precision.HIGHEST
EPSILON = 1e-05
MASK_FILL = 1000000000.0


def channel_scale():
    return (14 * WIN * WIN) ** (-0.5)


def to_tokens(glob_maps, loc_maps):
    channels = glob_maps.shape[-1]
    crop_count = glob_maps.shape[0]
    tiles = glob_maps.reshape(crop_count, 2, WIN, 2, WIN, channels).transpose(0, 1, 3, 2, 4, 5)
    return jnp.concatenate([tiles.reshape(-1, channels), loc_maps.reshape(-1, channels)], axis=0)


def to_maps(tokens, crop_count):
    channels = tokens.shape[-1]
    split_at = crop_count * 4 * WIN * WIN
    tiles = (
        tokens[:split_at].reshape(crop_count, 2, 2, WIN, WIN, channels).transpose(0, 1, 3, 2, 4, 5)
    )
    return (
        tiles.reshape(crop_count, 2 * WIN, 2 * WIN, channels),
        tokens[split_at:].reshape(-1, WIN, WIN, channels),
    )


def depthwise(map_data, kernel, offset):
    map_side = map_data.shape[1]
    padded = jnp.pad(map_data, ((0, 0), (1, 1), (1, 1), (0, 0)))
    result = jnp.zeros_like(map_data) + offset
    for tap_row in range(3):
        for tap_col in range(3):
            result = (
                result
                + padded[:, tap_row : tap_row + map_side, tap_col : tap_col + map_side, :]
                * kernel[3 * tap_row + tap_col]
            )
    return result


def conv_add(tokens, valid_mask, kernel, offset, crop_count):
    glob_maps, loc_maps = to_maps(tokens * valid_mask[:, None], crop_count)
    return tokens + to_tokens(
        depthwise(glob_maps, kernel, offset), depthwise(loc_maps, kernel, offset)
    )


def layer_norm(tokens, gain_vec, offset):
    centered = tokens - jnp.mean(tokens, axis=-1, keepdims=True)
    variance = jnp.mean(centered * centered, axis=-1, keepdims=True)
    return centered * lax.rsqrt(variance + EPSILON) * gain_vec + offset


def softmax_rows(scores):
    exponent = jnp.exp(scores - jnp.max(scores, axis=-1, keepdims=True))
    return exponent / jnp.sum(exponent, axis=-1, keepdims=True)


def gelu_exact(inputs):
    return 0.5 * inputs * (1.0 + lax.erf(inputs * 0.7071067811865476))


def local_mask(extent):
    cell_index = jnp.arange(WIN, dtype=jnp.int32)
    inside = (cell_index[None, :, None] < extent[:, 0, None, None]) & (
        cell_index[None, None, :] < extent[:, 1, None, None]
    )
    return inside.astype(jnp.float32).reshape(-1)


def dense(left_op, right_op):
    return jnp.dot(left_op, right_op, preferred_element_type=jnp.float32)


def weight_grad(inputs, upstream):
    return lax.dot_general(
        inputs, upstream, (((0,), (0,)), ((), ())), preferred_element_type=jnp.float32
    )


def input_grad(upstream, weight):
    return lax.dot_general(
        upstream, weight, (((1,), (1,)), ((), ())), preferred_element_type=jnp.float32
    )


def spatial_scores(queries, keys_in, key_bias):
    scores = jnp.einsum(
        "wnhc,wmhc->whnm", queries, keys_in, preferred_element_type=jnp.float32
    ) * HEAD_DIM ** (-0.5)
    return scores + key_bias[:, None, None, :]


def spatial_forward(projected, key_bias):
    channels = projected.shape[1] // 3
    windows = projected.shape[0] // (WIN * WIN)
    queries, keys_in, values = [
        projected[:, third_idx * channels : (third_idx + 1) * channels].reshape(
            windows, WIN * WIN, HEADS, HEAD_DIM
        )
        for third_idx in range(3)
    ]
    scores = spatial_scores(queries, keys_in, key_bias)
    row_max = jnp.max(scores, axis=-1, keepdims=True)
    exponent = jnp.exp(scores - row_max)
    row_sum = jnp.sum(exponent, axis=-1, keepdims=True)
    attn_probs = (exponent / row_sum).astype(jnp.bfloat16)
    attended = jnp.einsum(
        "whnm,wmhc->wnhc", attn_probs, values, preferred_element_type=jnp.float32
    ).astype(jnp.bfloat16)
    return (attended.reshape(-1, channels), (queries, keys_in, values, row_max + jnp.log(row_sum)))


def spatial_backward(grad_out, kept, key_bias):
    queries, keys_in, values, log_total = kept
    channels = grad_out.shape[1]
    attn_f32 = jnp.exp(spatial_scores(queries, keys_in, key_bias) - log_total)
    upstream = grad_out.reshape(values.shape)
    grad_probs = jnp.einsum("wnhc,wmhc->whnm", upstream, values, preferred_element_type=jnp.float32)
    grad_values = jnp.einsum(
        "whnm,wnhc->wmhc",
        attn_f32.astype(jnp.bfloat16),
        upstream,
        preferred_element_type=jnp.float32,
    )
    grad_scores = (
        attn_f32 * (grad_probs - jnp.sum(grad_probs * attn_f32, axis=-1, keepdims=True))
    ).astype(jnp.bfloat16)
    grad_queries = jnp.einsum(
        "whnm,wmhc->wnhc", grad_scores, keys_in, preferred_element_type=jnp.float32
    ) * HEAD_DIM ** (-0.5)
    grad_keys = jnp.einsum(
        "whnm,wnhc->wmhc", grad_scores, queries, preferred_element_type=jnp.float32
    ) * HEAD_DIM ** (-0.5)
    return jnp.concatenate(
        [member.reshape(-1, channels) for member in (grad_queries, grad_keys, grad_values)], axis=1
    ).astype(jnp.bfloat16)


def image_scores(masked, keys_in, image_hot, combine):
    gram_sums = jnp.einsum("wnhc,wnhd->whcd", masked, keys_in, preferred_element_type=jnp.float32)
    per_image = combine(jnp.einsum("wi,whcd->ihcd", image_hot, gram_sums, precision=PRECISE))
    return softmax_rows(per_image * channel_scale())


def apply_probs(attn_probs, values, image_hot):
    per_window = jnp.einsum(
        "wi,ihcd->whcd",
        image_hot.astype(jnp.bfloat16),
        attn_probs.astype(jnp.bfloat16),
        preferred_element_type=jnp.float32,
    ).astype(jnp.bfloat16)
    attended = jnp.einsum(
        "whcd,wnhd->wnhc", per_window, values, preferred_element_type=jnp.float32
    ).astype(jnp.bfloat16)
    return (attended, per_window)


def image_backward(upstream, masked, keys_in, values, attn_probs, per_window, image_hot, combine):
    grad_window = jnp.einsum(
        "wnhc,wnhd->whcd", upstream, values, preferred_element_type=jnp.float32
    )
    grad_image = combine(jnp.einsum("wi,whcd->ihcd", image_hot, grad_window, precision=PRECISE))
    grad_scores = (
        attn_probs * (grad_image - jnp.sum(grad_image * attn_probs, axis=-1, keepdims=True))
    ).astype(jnp.bfloat16)
    score_window = jnp.einsum(
        "wi,ihcd->whcd",
        image_hot.astype(jnp.bfloat16),
        grad_scores,
        preferred_element_type=jnp.float32,
    ).astype(jnp.bfloat16)
    grad_masked = (
        jnp.einsum("whcd,wnhd->wnhc", score_window, keys_in, preferred_element_type=jnp.float32)
        * channel_scale()
    ).astype(jnp.bfloat16)
    grad_keys = (
        jnp.einsum("whcd,wnhc->wnhd", score_window, masked, preferred_element_type=jnp.float32)
        * channel_scale()
    ).astype(jnp.bfloat16)
    grad_values = jnp.einsum(
        "whcd,wnhc->wnhd", per_window, upstream, preferred_element_type=jnp.float32
    ).astype(jnp.bfloat16)
    return (grad_masked, grad_keys, grad_values)


def keep_local(image_sum):
    return image_sum


def block_biases(shift_f, spatial):
    if spatial:
        return (
            jnp.concatenate([shift_f[4], jnp.zeros_like(shift_f[4]), shift_f[5]]),
            shift_f[6],
            shift_f[7],
        )
    return (shift_f[4:7].reshape(-1), shift_f[7], shift_f[8])


def block_forward(tokens, params, spatial, conv_at, attend):
    kernels, gain_rows, shifts, qkv_weight, proj_weight, fc1_weight, fc1_bias, fc2_weight = params
    kernel_f = kernels.astype(jnp.float32)
    gain_f = gain_rows.astype(jnp.float32)
    shift_f = shifts.astype(jnp.float32)
    qkv_bias, proj_bias, fc2_bias = block_biases(shift_f, spatial)
    section_one = conv_at(tokens, kernel_f[0], shift_f[0])
    normed = layer_norm(section_one, gain_f[0], shift_f[2]).astype(jnp.bfloat16)
    projected = (dense(normed, qkv_weight) + qkv_bias).astype(jnp.bfloat16)
    attended, attn_kept = attend(projected)
    section_two = section_one + dense(attended, proj_weight) + proj_bias
    section_three = conv_at(section_two, kernel_f[1], shift_f[1])
    normed_two = layer_norm(section_three, gain_f[1], shift_f[3]).astype(jnp.bfloat16)
    hidden_pre = dense(normed_two, fc1_weight) + fc1_bias.astype(jnp.float32)
    activated = gelu_exact(hidden_pre).astype(jnp.bfloat16)
    output = section_three + dense(activated, fc2_weight) + fc2_bias
    return (
        output,
        (
            tokens,
            section_one,
            normed,
            attn_kept,
            attended,
            section_two,
            section_three,
            normed_two,
            hidden_pre,
            activated,
        ),
    )


def block_backward(grad_out, kept, params, spatial, conv_at, attend_back):
    (
        tokens,
        section_one,
        normed,
        attn_kept,
        attended,
        section_two,
        section_three,
        normed_two,
        hidden_pre,
        activated,
    ) = kept
    kernels, gain_rows, shifts, qkv_weight, proj_weight, fc1_weight, fc1_bias, fc2_weight = params
    kernel_f = kernels.astype(jnp.float32)
    gain_f = gain_rows.astype(jnp.float32)
    shift_f = shifts.astype(jnp.float32)
    channels = grad_out.shape[1]
    grad_low = grad_out.astype(jnp.bfloat16)
    fc2_grad = weight_grad(activated, grad_low)
    fc2_bias_grad = jnp.sum(grad_low.astype(jnp.float32), axis=0)
    grad_act = input_grad(grad_low, fc2_weight)
    grad_hidden = jax.vjp(gelu_exact, hidden_pre)[1](grad_act)[0].astype(jnp.bfloat16)
    fc1_grad = weight_grad(normed_two, grad_hidden)
    fc1_bias_grad = jnp.sum(grad_hidden.astype(jnp.float32), axis=0)
    norm_pull = jax.vjp(layer_norm, section_three, gain_f[1], shift_f[3])[1]
    grad_three, gain1_grad, shift3_grad = norm_pull(input_grad(grad_hidden, fc1_weight))
    conv_pull = jax.vjp(conv_at, section_two, kernel_f[1], shift_f[1])[1]
    grad_two, kernel1_grad, shift1_grad = conv_pull(grad_out + grad_three)
    grad_attn = grad_two.astype(jnp.bfloat16)
    proj_grad = weight_grad(attended, grad_attn)
    proj_bias_grad = jnp.sum(grad_attn.astype(jnp.float32), axis=0)
    grad_attended = input_grad(grad_attn, proj_weight).astype(jnp.bfloat16)
    grad_proj = attend_back(grad_attended, attn_kept)
    qkv_grad = weight_grad(normed, grad_proj)
    bias_rows = jnp.sum(grad_proj.astype(jnp.float32), axis=0).reshape(3, channels)
    norm_pull_one = jax.vjp(layer_norm, section_one, gain_f[0], shift_f[2])[1]
    grad_one, gain0_grad, shift2_grad = norm_pull_one(input_grad(grad_proj, qkv_weight))
    conv_pull_one = jax.vjp(conv_at, tokens, kernel_f[0], shift_f[0])[1]
    grad_tokens, kernel0_grad, shift0_grad = conv_pull_one(grad_two + grad_one)
    if spatial:
        attn_rows = [bias_rows[0], bias_rows[2]]
    else:
        attn_rows = [bias_rows[0], bias_rows[1], bias_rows[2]]
    shift_grad = jnp.stack(
        [shift0_grad, shift1_grad, shift2_grad, shift3_grad]
        + attn_rows
        + [proj_bias_grad, fc2_bias_grad]
    )
    return (
        grad_tokens,
        (
            jnp.stack([kernel0_grad, kernel1_grad]),
            jnp.stack([gain0_grad, gain1_grad]),
            shift_grad,
            qkv_grad,
            proj_grad,
            fc1_grad,
            fc1_bias_grad,
            fc2_grad,
        ),
    )


def shards(
    glob_x,
    loc_x,
    glob_cot,
    loc_cot,
    loc_extent,
    glob_image,
    loc_image,
    s_kernels,
    s_gains,
    s_shifts,
    s_qkv,
    s_proj,
    s_fc1,
    s_fc1_bias,
    s_fc2,
    c_kernels,
    c_gains,
    c_shifts,
    c_qkv,
    c_proj,
    c_fc1,
    c_fc1_bias,
    c_fc2,
):
    crop_count = glob_x.shape[0]
    local_count = loc_x.shape[0]
    tokens = to_tokens(glob_x, loc_x).astype(jnp.float32)
    valid_mask = jnp.concatenate(
        [jnp.ones((crop_count * 4 * WIN * WIN,), jnp.float32), local_mask(loc_extent)]
    )
    valid_low = valid_mask.astype(jnp.bfloat16)
    key_bias = (valid_mask.reshape(-1, WIN * WIN) - 1.0) * MASK_FILL
    group_count = lax.axis_size("grp")
    row_images = glob_image.shape[0] // 2
    image_table = jnp.concatenate(
        [
            jnp.repeat(glob_image.reshape(group_count, crop_count), 4, axis=1),
            loc_image.reshape(group_count, local_count),
        ],
        axis=1,
    )
    image_range = jnp.arange(row_images, dtype=jnp.int32)
    row_hot = (image_table.reshape(-1)[:, None] == image_range[None, :]).astype(jnp.float32)

    def conv_at(inputs, kernel, offset):
        return conv_add(inputs, valid_mask, kernel, offset, crop_count)

    def spatial_attend(projected):
        return spatial_forward(projected, key_bias)

    def spatial_back(grad_out, kept):
        return spatial_backward(grad_out, kept, key_bias)

    def channel_attend(projected):
        channels = projected.shape[1] // 3
        masked = projected[:, :channels] * valid_low[:, None]
        keys_in = projected[:, channels : 2 * channels]
        values = projected[:, 2 * channels :]
        recv_query, recv_key, recv_value = (
            lax.all_to_all(masked, "grp", split_axis=1, concat_axis=0, tiled=True),
            lax.all_to_all(keys_in, "grp", split_axis=1, concat_axis=0, tiled=True),
            lax.all_to_all(values, "grp", split_axis=1, concat_axis=0, tiled=True),
        )
        piece_width = recv_query.shape[1]
        shaped = [
            member.reshape(-1, WIN * WIN, piece_width // HEAD_DIM, HEAD_DIM)
            for member in (recv_query, recv_key, recv_value)
        ]
        attn_probs = image_scores(shaped[0], shaped[1], row_hot, keep_local)
        attended, per_window = apply_probs(attn_probs, shaped[2], row_hot)
        result = lax.all_to_all(
            attended.reshape(-1, piece_width), "grp", split_axis=0, concat_axis=1, tiled=True
        )
        return (result, (shaped, attn_probs, per_window))

    def channel_back(grad_out, kept):
        shaped, attn_probs, per_window = kept
        channels = grad_out.shape[1]
        upstream = lax.all_to_all(grad_out, "grp", split_axis=1, concat_axis=0, tiled=True).reshape(
            shaped[0].shape
        )
        grads_back = image_backward(
            upstream, shaped[0], shaped[1], shaped[2], attn_probs, per_window, row_hot, keep_local
        )
        piece_width = shaped[0].shape[2] * HEAD_DIM
        back_query, back_key, back_value = (
            lax.all_to_all(
                grads_back[0].reshape(-1, piece_width),
                "grp",
                split_axis=0,
                concat_axis=1,
                tiled=True,
            ),
            lax.all_to_all(
                grads_back[1].reshape(-1, piece_width),
                "grp",
                split_axis=0,
                concat_axis=1,
                tiled=True,
            ),
            lax.all_to_all(
                grads_back[2].reshape(-1, piece_width),
                "grp",
                split_axis=0,
                concat_axis=1,
                tiled=True,
            ),
        )
        return jnp.concatenate([back_query * valid_low[:, None], back_key, back_value], axis=1)

    s_params = (s_kernels, s_gains, s_shifts, s_qkv, s_proj, s_fc1, s_fc1_bias, s_fc2)
    c_params = (c_kernels, c_gains, c_shifts, c_qkv, c_proj, c_fc1, c_fc1_bias, c_fc2)
    middle, s_kept = block_forward(tokens, s_params, True, conv_at, spatial_attend)
    output, c_kept = block_forward(middle, c_params, False, conv_at, channel_attend)
    glob_out, loc_out = to_maps(output, crop_count)
    upstream = to_tokens(glob_cot, loc_cot).astype(jnp.float32)
    grad_middle, c_grads = block_backward(upstream, c_kept, c_params, False, conv_at, channel_back)
    grad_tokens, s_grads = block_backward(
        grad_middle, s_kept, s_params, True, conv_at, spatial_back
    )
    glob_grad, loc_grad = to_maps(grad_tokens, crop_count)
    shares = (
        lax.psum_scatter(
            s_grads[0].astype(jnp.bfloat16), "grp", scatter_dimension=2, tiled=True
        ).astype(jnp.float32),
        lax.psum_scatter(
            s_grads[1].astype(jnp.bfloat16), "grp", scatter_dimension=1, tiled=True
        ).astype(jnp.float32),
        lax.psum_scatter(
            s_grads[2].astype(jnp.bfloat16), "grp", scatter_dimension=1, tiled=True
        ).astype(jnp.float32),
        lax.psum_scatter(
            s_grads[3].astype(jnp.bfloat16), "grp", scatter_dimension=1, tiled=True
        ).astype(jnp.float32),
        lax.psum_scatter(
            s_grads[4].astype(jnp.bfloat16), "grp", scatter_dimension=1, tiled=True
        ).astype(jnp.float32),
        lax.psum_scatter(
            s_grads[5].astype(jnp.bfloat16), "grp", scatter_dimension=1, tiled=True
        ).astype(jnp.float32),
        lax.psum_scatter(
            s_grads[6].astype(jnp.bfloat16), "grp", scatter_dimension=0, tiled=True
        ).astype(jnp.float32),
        lax.psum_scatter(
            s_grads[7].astype(jnp.bfloat16), "grp", scatter_dimension=1, tiled=True
        ).astype(jnp.float32),
        lax.psum_scatter(
            c_grads[0].astype(jnp.bfloat16), "grp", scatter_dimension=2, tiled=True
        ).astype(jnp.float32),
        lax.psum_scatter(
            c_grads[1].astype(jnp.bfloat16), "grp", scatter_dimension=1, tiled=True
        ).astype(jnp.float32),
        lax.psum_scatter(
            c_grads[2].astype(jnp.bfloat16), "grp", scatter_dimension=1, tiled=True
        ).astype(jnp.float32),
        lax.psum_scatter(
            c_grads[3].astype(jnp.bfloat16), "grp", scatter_dimension=1, tiled=True
        ).astype(jnp.float32),
        lax.psum_scatter(
            c_grads[4].astype(jnp.bfloat16), "grp", scatter_dimension=1, tiled=True
        ).astype(jnp.float32),
        lax.psum_scatter(
            c_grads[5].astype(jnp.bfloat16), "grp", scatter_dimension=1, tiled=True
        ).astype(jnp.float32),
        lax.psum_scatter(
            c_grads[6].astype(jnp.bfloat16), "grp", scatter_dimension=0, tiled=True
        ).astype(jnp.float32),
        lax.psum_scatter(
            c_grads[7].astype(jnp.bfloat16), "grp", scatter_dimension=1, tiled=True
        ).astype(jnp.float32),
    )
    totals = (
        lax.psum(shares[0].astype(jnp.bfloat16), "img").astype(jnp.float32),
        lax.psum(shares[1].astype(jnp.bfloat16), "img").astype(jnp.float32),
        lax.psum(shares[2].astype(jnp.bfloat16), "img").astype(jnp.float32),
        lax.psum(shares[3].astype(jnp.bfloat16), "img").astype(jnp.float32),
        lax.psum(shares[4].astype(jnp.bfloat16), "img").astype(jnp.float32),
        lax.psum(shares[5].astype(jnp.bfloat16), "img").astype(jnp.float32),
        lax.psum(shares[6].astype(jnp.bfloat16), "img").astype(jnp.float32),
        lax.psum(shares[7].astype(jnp.bfloat16), "img").astype(jnp.float32),
        lax.psum(shares[8].astype(jnp.bfloat16), "img").astype(jnp.float32),
        lax.psum(shares[9].astype(jnp.bfloat16), "img").astype(jnp.float32),
        lax.psum(shares[10].astype(jnp.bfloat16), "img").astype(jnp.float32),
        lax.psum(shares[11].astype(jnp.bfloat16), "img").astype(jnp.float32),
        lax.psum(shares[12].astype(jnp.bfloat16), "img").astype(jnp.float32),
        lax.psum(shares[13].astype(jnp.bfloat16), "img").astype(jnp.float32),
        lax.psum(shares[14].astype(jnp.bfloat16), "img").astype(jnp.float32),
        lax.psum(shares[15].astype(jnp.bfloat16), "img").astype(jnp.float32),
    )
    return (
        glob_out.astype(jnp.bfloat16),
        loc_out.astype(jnp.bfloat16),
        glob_grad,
        loc_grad,
        totals[0],
        totals[1],
        totals[2],
        totals[3],
        totals[4],
        totals[5],
        totals[6],
        totals[7],
        totals[8],
        totals[9],
        totals[10],
        totals[11],
        totals[12],
        totals[13],
        totals[14],
        totals[15],
    )


def solution(mesh):
    return jax.shard_map(
        shards,
        mesh=mesh,
        in_specs=(
            P(("img", "grp"), None, None, None),
            P(("img", "grp"), None, None, None),
            P(("img", "grp"), None, None, None),
            P(("img", "grp"), None, None, None),
            P(("img", "grp"), None),
            P("img"),
            P("img"),
            P(),
            P(),
            P(),
            P(),
            P(),
            P(),
            P(),
            P(),
            P(),
            P(),
            P(),
            P(),
            P(),
            P(),
            P(),
            P(),
        ),
        out_specs=(
            P(("img", "grp"), None, None, None),
            P(("img", "grp"), None, None, None),
            P(("img", "grp"), None, None, None),
            P(("img", "grp"), None, None, None),
            P(None, None, "grp"),
            P(None, "grp"),
            P(None, "grp"),
            P(None, "grp"),
            P(None, "grp"),
            P(None, "grp"),
            P("grp"),
            P(None, "grp"),
            P(None, None, "grp"),
            P(None, "grp"),
            P(None, "grp"),
            P(None, "grp"),
            P(None, "grp"),
            P(None, "grp"),
            P("grp"),
            P(None, "grp"),
        ),
        check_vma=False,
    )
```

profile of v0, /device:TPU:0, one launch (start us, length us, event | category | flops | bytes accessed | tf_op | source)
XLA Modules:
  0.0 1340.0 jit_solution(15605644546213102401)
XLA Ops:
  50.5 7.3 reshape.1123
  57.8 8.6 copy.220
  66.5 19.1 %reshape.1122 = bf16[28,49,16,32]{3,2,1,0:T(8,128)(2,1)} reshape(bf16[1372,512]{1,0:T(8,128)(2,1)} %get-tuple-element.208) | data formatting | bytes 2809856 | tf_op jit(solution)/shard_map/reshape | solution.py:110
  85.6 8.6 copy.219
  99.7 8.6 copy.221
  108.3 12.7 fusion.100
  120.9 8.7 fusion.1
  129.7 7.4 convert_bitcast_fusion.3
  141.9 7.0 reshape.1037
  181.5 7.2 multiply_convert_fusion.2
  237.9 32.5 %all-to-all-done = bf16[1372,8,64]{0,2,1:T(8,128)(2,1)S(1)} async-done(((bf16[1372,8,64]{0,2,1:T(8,128)(2,1)}), bf16[1372,8,64]{0,2,1:T(8,128)(2,1)S(1)}, u32[]{:S(2)}, u32[]{:S(2)}) %all-to-all-start) | async-done | bytes 1404960 | tf_op jit(solution)/shard_map/all_to_all | solution.py:372
  277.3 32.5 %all-to-all-done.2 = bf16[1372,8,64]{0,2,1:T(8,128)(2,1)} async-done(((bf16[1372,8,64]{0,2,1:T(8,128)(2,1)}), bf16[1372,8,64]{0,2,1:T(8,128)(2,1)}, u32[]{:S(2)}, u32[]{:S(2)}) %all-to-all-start.2) | async-done | bytes 1404960 | tf_op jit(solution)/shard_map/all_to_all | solution.py:371
  328.5 20.5 %all-to-all-done.1 = bf16[1372,8,64]{0,2,1:T(8,128)(2,1)} async-done(((bf16[1372,8,64]{0,2,1:T(8,128)(2,1)}), bf16[1372,8,64]{0,2,1:T(8,128)(2,1)}, u32[]{:S(2)}, u32[]{:S(2)}) %all-to-all-start.1) | async-done | bytes 1404960 | tf_op jit(solution)/shard_map/all_to_all | solution.py:370
  370.7 6.6 fusion.47
  381.5 6.6 copy.264
  418.4 24.2 %all-to-all-done.3 = bf16[8,1372,64]{1,2,0:T(8,128)(2,1)S(1)} async-done(((bf16[8,1372,64]{1,2,0:T(8,128)(2,1)}), bf16[8,1372,64]{1,2,0:T(8,128)(2,1)S(1)}, u32[]{:S(2)}, u32[]{:S(2)}) %all-to-all-start.3) | async-done | bytes 1404960 | tf_op jit(solution)/shard_map/all_to_all | solution.py:381
  480.5 10.1 fusion.103
  533.1 37.4 %all_to_all.140 = bf16[1372,8,64]{0,2,1:T(8,128)(2,1)S(1)} all-to-all(bf16[1372,8,64]{0,2,1:T(8,128)(2,1)S(1)} %bitcast.380), channel_id=1, replica_groups=mesh['img'=4,'grp'=8] {'grp'}, dimensions={1} | all-to-all | bytes 2809856 | tf_op jit(solution)/shard_map/all_to_all | solution.py:389
  603.7 7.3 multiply_reduce_fusion.85
  640.8 7.8 convolution_convert_fusion.4
  666.5 20.3 %all-to-all-done.5 = bf16[8,1372,64]{1,2,0:T(8,128)(2,1)S(1)} async-done(((bf16[8,1372,64]{1,2,0:T(8,128)(2,1)}), bf16[8,1372,64]{1,2,0:T(8,128)(2,1)S(1)}, u32[]{:S(2)}, u32[]{:S(2)}) %all-to-all-start.5) | async-done | bytes 1404960 | tf_op jit(solution)/shard_map/all_to_all | solution.py:397
  691.9 8.5 convolution_convert_fusion.5
  703.3 35.4 %all-to-all-done.6 = bf16[8,1372,64]{1,2,0:T(8,128)(2,1)} async-done(((bf16[8,1372,64]{1,2,0:T(8,128)(2,1)}), bf16[8,1372,64]{1,2,0:T(8,128)(2,1)}, u32[]{:S(2)}, u32[]{:S(2)}) %all-to-all-start.6) | async-done | bytes 1404960 | tf_op jit(solution)/shard_map/all_to_all | solution.py:404
  741.3 6.6 multiply_reduce_fusion.2
  769.4 6.5 multiply_reduce_fusion.32
  784.4 11.8 fusion.102
  848.8 8.9 copy.274
  865.0 15.5 %multiply_reduce_fusion = (f32[28,16,49]{2,1,0:T(8,128)S(1)}, f32[28,16,49,49]{2,3,1,0:T(8,128)}) fusion(f32[28,16,49,49]{2,3,1,0:T(8,128)} %get-tuple-element.358, f32[28,16,49]{2,1,0:T(8,128)S(1)} %copy-done.84, bf16[28,49,16,32]{1,3,2,0:T(8,128)(2,1)} %copy.274, bf16[28,49,16,32]{1,3,2,0:T(8,128)(2,1)} %copy.221), kind=kOutput, calls=%fused_computation.2 | convolution fusion | flops 72046464 | bytes 11590656 | tf_op jit(solution)/shard_map/wnhc,wmhc->whnm/dot_general | solution.py:131
  880.5 13.0 multiply_convert_fusion
  893.6 11.1 convert_bitcast_fusion
  911.1 7.1 reshape.1087
  928.5 7.0 reshape.1085
  935.4 7.4 fusion.16
  947.3 8.0 reshape.1086
  964.2 8.2 convolution_convert_fusion.6
  979.3 6.8 multiply_reduce_fusion.4
  988.9 7.7 convolution_convert_fusion.7
  1024.9 6.5 multiply_reduce_fusion.48
  1041.4 7.2 fusion.35
  1053.9 17.6 %reduce-scatter.31.cloned.1.call-done = bf16[512,256]{1,0:T(8,128)(2,1)} async-done(((bf16[512,2048]{1,0:T(8,128)(2,1)}), bf16[512,256]{1,0:T(8,128)(2,1)}) %reduce-scatter.31.cloned.1.call-update) | async-done | bytes 262160 | tf_op jit(solution)/shard_map/reduce_scatter | solution.py:448
  1090.4 15.1 %all-reduce.163 = (bf16[2048]{0:T(1024)(128)(2,1)S(1)}, bf16[2048]{0:T(1024)(128)(2,1)S(1)}) all-reduce(bf16[2048]{0:T(1024)(128)(2,1)S(1)} %copy-done.279, bf16[2048]{0:T(1024)(128)(2,1)S(1)} %copy-done.278), channel_id=8, replica_groups=mesh['img'=4,'grp'=8] {'grp'}, use_global_device_ids=true, to_apply=%region_82.83.clone | all-reduce | flops 4096 | bytes 16384
  1113.1 21.2 %reduce-scatter.45.cloned.1.call-done = bf16[64,2]{1,0:T(8,128)(2,1)} async-done(((bf16[512,2]{1,0:T(8,128)(2,1)}), bf16[64,2]{1,0:T(8,128)(2,1)}) %reduce-scatter.45.cloned.1.call-update) | async-done | bytes 272
  1135.1 30.3 %reduce-scatter.47.cloned.1.call-done = bf16[64,8]{1,0:T(8,128)(2,1)} async-done(((bf16[512,8]{1,0:T(8,128)(2,1)}), bf16[64,8]{1,0:T(8,128)(2,1)}) %reduce-scatter.47.cloned.1.call-update) | async-done | bytes 1040
  1166.2 30.4 %reduce-scatter.53.cloned.1.call-done = bf16[64,9]{1,0:T(8,128)(2,1)} async-done(((bf16[512,9]{1,0:T(8,128)(2,1)}), bf16[64,9]{1,0:T(8,128)(2,1)}) %reduce-scatter.53.cloned.1.call-update) | async-done | bytes 1168
  1197.3 30.4 %reduce-scatter.49.cloned.1.call-done = bf16[64,18]{1,0:T(8,128)(2,1)} async-done(((bf16[512,18]{1,0:T(8,128)(2,1)}), bf16[64,18]{1,0:T(8,128)(2,1)}) %reduce-scatter.49.cloned.1.call-update) | async-done | bytes 2320
  1228.7 30.2 %reduce-scatter.43.cloned.1.call-done = bf16[64,18]{1,0:T(8,128)(2,1)} async-done(((bf16[512,18]{1,0:T(8,128)(2,1)}), bf16[64,18]{1,0:T(8,128)(2,1)}) %reduce-scatter.43.cloned.1.call-update) | async-done | bytes 2320
  1259.8 16.6 %all-reduce.164 = (bf16[2,9,64]{2,1,0:T(8,128)(2,1)S(1)}, bf16[2,9,64]{2,1,0:T(8,128)(2,1)S(1)}, bf16[2,64]{1,0:T(2,128)(2,1)S(1)}, bf16[8,64]{1,0:T(8,128)(2,1)...) all-reduce(bf16[2,9,64]{2,1,0:T(8,128)(2,1)S(1)} %copy.297, ...), channel_id=1, replica_groups=mesh['img'=4,'grp'=8] {'img'}, use_global_device_ids=true, to_apply=%region_59.60 | all-reduce | flops 4160 | bytes 16640 | tf_op jit(solution)/shard_map/psum | solution.py:483
  1281.1 42.2 %all-reduce.168.cloned.1.call-done = (bf16[512,192]{0,1:T(8,128)(2,1)}, bf16[512,64]{0,1:T(8,128)(2,1)}, bf16[512,256]{1,0:T(8,128)(2,1)}, bf16[2048,64]{0,1:T(8...) async-done(((bf16[512,192]{0,1:T(8,128)(2,1)}, bf16[512,64]{0,1:T(8,128)(2,1)}, ...) | async-done | bytes 1572880 | tf_op jit(solution)/shard_map/psum | solution.py:486
  (982 shorter events, 602.5 us)
Async XLA Ops:
  7.2 466.8 %copy-start = (bf16[512,2048]{1,0:T(8,128)(2,1)S(1)}, bf16[512,2048]{1,0:T(8,128)(2,1)}, u32[]{:S(2)}) copy-start(bf16[512,2048]{1,0:T(8,128)(2,1)} %param.43) | copy-start | bytes 6291460
  21.2 147.3 %copy-start.135 = (f32[1,1,512]{2,0,1:T(1,128)}, f32[1,1,512]{2,0,1:T(1,128)S(1)}, u32[]{:S(2)}) copy-start(f32[1,1,512]{2,0,1:T(1,128)S(1)} %get-tuple-element.312) | copy-start | bytes 6148
  21.2 147.3 %copy-start.137 = (f32[1,1,512]{2,0,1:T(1,128)}, f32[1,1,512]{2,0,1:T(1,128)S(1)}, u32[]{:S(2)}) copy-start(f32[1,1,512]{2,0,1:T(1,128)S(1)} %get-tuple-element.313) | copy-start | bytes 6148
  156.5 23.0 %copy-start.267 = (f32[2048]{0:T(1024)}, f32[2048]{0:T(1024)S(1)}, u32[]{:S(2)}) copy-start(f32[2048]{0:T(1024)S(1)} %convert_element_type.322) | copy-start | bytes 24580
  196.7 23.7 %copy-start.209 = (f32[1,512]{1,0:T(1,128)}, f32[1,512]{1,0:T(1,128)S(1)}, u32[]{:S(2)}) copy-start(f32[1,512]{1,0:T(1,128)S(1)} %get-tuple-element.350) | copy-start | bytes 6148
  197.4 11.9 copy-start.159
  197.4 11.9 copy-start.161
  197.4 11.9 copy-start.163
  197.4 11.9 copy-start.165
  197.4 265.3 %copy-start.171 = (f32[1,1,512]{2,0,1:T(1,128)}, f32[1,1,512]{2,0,1:T(1,128)S(1)}, u32[]{:S(2)}) copy-start(f32[1,1,512]{2,0,1:T(1,128)S(1)} %get-tuple-element.294) | copy-start | bytes 6148
  197.4 265.3 %copy-start.173 = (f32[1,1,512]{2,0,1:T(1,128)}, f32[1,1,512]{2,0,1:T(1,128)S(1)}, u32[]{:S(2)}) copy-start(f32[1,1,512]{2,0,1:T(1,128)S(1)} %get-tuple-element.295) | copy-start | bytes 6148
  229.0 41.4 %all-to-all-start = ((bf16[1372,8,64]{0,2,1:T(8,128)(2,1)}), bf16[1372,8,64]{0,2,1:T(8,128)(2,1)S(1)}, u32[]{:S(2)}, u32[]{:S(2)}) async-start(bf16[1372,8,64]{0,2,1:T(8,128)(2,1)} %bitcast.379), calls=%async_computation | async-start | bytes 2883584 | tf_op jit(solution)/shard_map/all_to_all | solution.py:372
  270.4 39.3 %all-to-all-start.2 = ((bf16[1372,8,64]{0,2,1:T(8,128)(2,1)}), bf16[1372,8,64]{0,2,1:T(8,128)(2,1)}, u32[]{:S(2)}, u32[]{:S(2)}) async-start(bf16[1372,8,64]{0,2,1:T(8,128)(2,1)} %bitcast.378), calls=%async_computation.2 | async-start | bytes 2883584 | tf_op jit(solution)/shard_map/all_to_all | solution.py:371
  309.7 39.3 %all-to-all-start.1 = ((bf16[1372,8,64]{0,2,1:T(8,128)(2,1)}), bf16[1372,8,64]{0,2,1:T(8,128)(2,1)}, u32[]{:S(2)}, u32[]{:S(2)}) async-start(bf16[1372,8,64]{0,2,1:T(8,128)(2,1)} %bitcast.377), calls=%async_computation.1 | async-start | bytes 2883584 | tf_op jit(solution)/shard_map/all_to_all | solution.py:370
  404.0 38.5 %all-to-all-start.3 = ((bf16[8,1372,64]{1,2,0:T(8,128)(2,1)}), bf16[8,1372,64]{1,2,0:T(8,128)(2,1)S(1)}, u32[]{:S(2)}, u32[]{:S(2)}) async-start(bf16[8,1372,64]{1,2,0:T(8,128)(2,1)} %copy.242), calls=%async_computation.3 | async-start | bytes 2883584 | tf_op jit(solution)/shard_map/all_to_all | solution.py:381
  473.4 21.8 %copy-start.13 = (f32[1372,512]{1,0:T(8,128)}, f32[1372,512]{1,0:T(8,128)S(1)}, u32[]{:S(2)}) copy-start(f32[1372,512]{1,0:T(8,128)S(1)} %get-tuple-element.197) | copy-start | bytes 8429572
  474.0 21.2 %copy-start.192 = (f32[1372]{0:T(1024)}, f32[1372]{0:T(1024)S(1)}, u32[]{:S(2)}) copy-start(f32[1372]{0:T(1024)S(1)} %fusion.70) | copy-start | bytes 16468
  590.2 45.4 %all-to-all-start.7 = ((bf16[8,1372,64]{1,2,0:T(8,128)(2,1)}), bf16[8,1372,64]{1,2,0:T(8,128)(2,1)S(1)}, u32[]{:S(2)}, u32[]{:S(2)}) async-start(bf16[8,1372,64]{1,2,0:T(8,128)(2,1)} %copy.266), calls=%async_computation.7 | async-start | bytes 2883584 | tf_op jit(solution)/shard_map/all_to_all | solution.py:411
  593.9 459.9 %reduce-scatter.37.cloned.1.call-start = ((), (), s32[]{:S(2)}) async-start(), calls=%async_computation.27 | async-start | bytes 589824 | tf_op jit(solution)/shard_map/reduce_scatter | solution.py:469
  635.6 51.2 %all-to-all-start.5 = ((bf16[8,1372,64]{1,2,0:T(8,128)(2,1)}), bf16[8,1372,64]{1,2,0:T(8,128)(2,1)S(1)}, u32[]{:S(2)}, u32[]{:S(2)}) async-start(bf16[8,1372,64]{1,2,0:T(8,128)(2,1)} %copy.257), calls=%async_computation.5 | async-start | bytes 2883584 | tf_op jit(solution)/shard_map/all_to_all | solution.py:397
  640.6 413.2 %reduce-scatter.41.cloned.1.call-start = ((), (), s32[]{:S(2)}) async-start(), calls=%async_computation.29 | async-start | bytes 2359296 | tf_op jit(solution)/shard_map/reduce_scatter | solution.py:478
  666.5 24.7 %copy-start.93 = (f32[28,16,49]{2,1,0:T(8,128)S(1)}, f32[28,16,49]{2,1,0:T(8,128)}, u32[]{:S(2)}) copy-start(f32[28,16,49]{2,1,0:T(8,128)} %copy-done.92) | copy-start | bytes 263428
  666.5 24.7 %copy-start.95 = (f32[28,16,49]{2,1,0:T(8,128)S(1)}, f32[28,16,49]{2,1,0:T(8,128)}, u32[]{:S(2)}) copy-start(f32[28,16,49]{2,1,0:T(8,128)} %copy-done.94) | copy-start | bytes 263428
  666.5 25.4 %copy-start.193 = (f32[1372]{0:T(1024)S(1)}, f32[1372]{0:T(1024)}, u32[]{:S(2)}) copy-start(f32[1372]{0:T(1024)} %copy-done.192) | copy-start | bytes 16468
  666.5 25.4 %copy-start.213 = (f32[1,512]{1,0:T(1,128)S(1)}, f32[1,512]{1,0:T(1,128)}, u32[]{:S(2)}) copy-start(f32[1,512]{1,0:T(1,128)} %get-tuple-element.349) | copy-start | bytes 6148
  666.5 25.4 %copy-start.288 = (f32[1,512]{1,0:T(1,128)S(1)}, f32[1,512]{1,0:T(1,128)}, u32[]{:S(2)}) copy-start(f32[1,512]{1,0:T(1,128)} %get-tuple-element.331) | copy-start | bytes 6148
  686.8 51.9 %all-to-all-start.6 = ((bf16[8,1372,64]{1,2,0:T(8,128)(2,1)}), bf16[8,1372,64]{1,2,0:T(8,128)(2,1)}, u32[]{:S(2)}, u32[]{:S(2)}) async-start(bf16[8,1372,64]{1,2,0:T(8,128)(2,1)} %copy.262), calls=%async_computation.6 | async-start | bytes 2883584 | tf_op jit(solution)/shard_map/all_to_all | solution.py:404
  691.1 362.7 %reduce-scatter.39.cloned.1.call-start = ((), (), s32[]{:S(2)}) async-start(), calls=%async_computation.28 | async-start | bytes 2359296 | tf_op jit(solution)/shard_map/reduce_scatter | solution.py:472
  700.5 353.4 %reduce-scatter.29.cloned.1.call-start = ((), (), s32[]{:S(2)}) async-start(), calls=%async_computation.23 | async-start | bytes 589824 | tf_op jit(solution)/shard_map/reduce_scatter | solution.py:445
  703.2 44.7 %copy-start.65 = (bf16[1372,512]{1,0:T(8,128)(2,1)}, bf16[1372,512]{1,0:T(8,128)(2,1)S(1)}, u32[]{:S(2)}) copy-start(bf16[1372,512]{1,0:T(8,128)(2,1)S(1)} %broadcast_multiply_fusion.39) | copy-start | bytes 4214788
  703.3 38.0 %copy-start.63 = (bf16[1372,512]{1,0:T(8,128)(2,1)S(1)}, bf16[1372,512]{1,0:T(8,128)(2,1)}, u32[]{:S(2)}) copy-start(bf16[1372,512]{1,0:T(8,128)(2,1)} %copy.268) | copy-start | bytes 4214788
  703.3 38.0 %copy-start.108 = (f32[1372]{0:T(1024)S(1)}, f32[1372]{0:T(1024)}, u32[]{:S(2)}) copy-start(f32[1372]{0:T(1024)} %copy-done.107) | copy-start | bytes 16468
  703.3 38.0 %copy-start.190 = (f32[1372]{0:T(1024)S(1)}, f32[1372]{0:T(1024)}, u32[]{:S(2)}) copy-start(f32[1372]{0:T(1024)} %copy-done.189) | copy-start | bytes 16468
  703.3 38.0 %copy-start.210 = (f32[1,512]{1,0:T(1,128)S(1)}, f32[1,512]{1,0:T(1,128)}, u32[]{:S(2)}) copy-start(f32[1,512]{1,0:T(1,128)} %copy-done.209) | copy-start | bytes 6148
  784.3 17.7 %copy-start.47 = (f32[1372,512]{1,0:T(8,128)}, f32[1372,512]{1,0:T(8,128)S(1)}, u32[]{:S(2)}) copy-start(f32[1372,512]{1,0:T(8,128)S(1)} %get-tuple-element.185) | copy-start | bytes 8429572
  840.6 213.3 %reduce-scatter.35.cloned.1.call-start = ((), (), s32[]{:S(2)}) async-start(), calls=%async_computation.26 | async-start | bytes 1769472 | tf_op jit(solution)/shard_map/reduce_scatter | solution.py:466
  864.1 189.8 %reduce-scatter.27.cloned.1.call-start = ((), (), s32[]{:S(2)}) async-start(), calls=%async_computation.22 | async-start | bytes 1769472 | tf_op jit(solution)/shard_map/reduce_scatter | solution.py:442
  964.2 89.7 %reduce-scatter.33.cloned.1.call-start = ((), (), s32[]{:S(2)}) async-start(), calls=%async_computation.25 | async-start | bytes 2359296 | tf_op jit(solution)/shard_map/reduce_scatter | solution.py:454
  972.5 99.0 %reduce-scatter.31.cloned.1.call-start = ((), (), s32[]{:S(2)}) async-start(), calls=%async_computation.24 | async-start | bytes 2359296 | tf_op jit(solution)/shard_map/reduce_scatter | solution.py:448
  996.6 115.7 %reduce-scatter.51.cloned.1.call-start = ((), (), s32[]{:S(2)}) async-start(), calls=%async_computation.34 | async-start | bytes 147456
  1031.4 102.9 %reduce-scatter.45.cloned.1.call-start = ((), (), s32[]{:S(2)}) async-start(), calls=%async_computation.31 | async-start | bytes 147456
  1035.7 129.7 %reduce-scatter.47.cloned.1.call-start = ((), (), s32[]{:S(2)}) async-start(), calls=%async_computation.32 | async-start | bytes 147456
  1037.4 159.1 %reduce-scatter.53.cloned.1.call-start = ((), (), s32[]{:S(2)}) async-start(), calls=%async_computation.35 | async-start | bytes 147456
  1038.4 189.3 %reduce-scatter.49.cloned.1.call-start = ((), (), s32[]{:S(2)}) async-start(), calls=%async_computation.33 | async-start | bytes 147456
  1039.8 219.1 %reduce-scatter.43.cloned.1.call-start = ((), (), s32[]{:S(2)}) async-start(), calls=%async_computation.30 | async-start | bytes 147456
  1041.2 282.1 %all-reduce.168.cloned.1.call-start = ((), (), s32[]{:S(2)}) async-start(), calls=%async_computation.36 | async-start | bytes 3145728 | tf_op jit(solution)/shard_map/psum | solution.py:486
  1050.9 20.6 %copy-start.78 = (f32[12,7,7,512]{3,2,1,0:T(8,128)S(1)}, f32[12,7,7,512]{3,2,1,0:T(8,128)}, u32[]{:S(2)}) copy-start(f32[12,7,7,512]{3,2,1,0:T(8,128)} %get-tuple-element.282) | copy-start | bytes 3612676
  1090.4 16.5 %slice-start = ((f32[1372,512]{1,0:T(8,128)}), f32[784,512]{1,0:T(8,128)S(1)}, s32[]{:S(2)}) async-start(f32[1372,512]{1,0:T(8,128)} %copy-done.48), calls=%async_computation.37 | async-start | bytes 3211264 | tf_op jit(solution)/shard_map/slice | solution.py:31
  (282 other events, 1186.5 us)
Sparse Core Ops, SparseCore 0:
  597.9 35.5 reduce-scatter.36
  648.7 47.3 reduce-scatter.40
  700.6 47.8 reduce-scatter.38
  840.7 30.9 reduce-scatter.28
  873.9 32.4 reduce-scatter.34
  964.3 33.9 reduce-scatter.26
  1000.6 34.1 reduce-scatter.32
  1037.1 34.4 reduce-scatter.30
  1074.4 28.8 reduce-scatter.50
  1106.0 28.2 reduce-scatter.44
  1137.1 28.2 reduce-scatter.46
  1168.2 28.3 reduce-scatter.52
  1199.4 28.3 reduce-scatter.48
  1230.5 28.3 reduce-scatter.42
  1262.6 60.7 all-reduce.167
where the time goes:
time: 1350 us; the launch traced here: 1340 us
  local copies, waits for them, and re-layouts  399 us (30%)
  waiting for transfers between devices  368 us (27%)
  matrix products  251 us (19%)
  other arithmetic  201 us (15%)
  blocking collectives  69.1 us (5%)
  starting transfers between devices  32.8 us (2%)
  between operations  19.1 us (1%)
    unnamed x21, waiting for transfers between devices  143 us
    reshape x6, local copies, waits for them, and re-layouts, spatial_forward(): projected[:, third_idx * channels:(third_idx + 1) * channels]  57.7 us
    dot_general x8, matrix products, input_grad(): lax.dot_general(upstream, weight, (((1,), (1,)), ((), ())), preferred_ele...  48.1 us
    dot_general x8, matrix products, weight_grad(): lax.dot_general(inputs, upstream, (((0,), (0,)), ((), ())), preferred_ele...  48 us
    unnamed x638, local copies, waits for them, and re-layouts  43.6 us
    reduce_sum x12, other arithmetic, depthwise(): padded[:, tap_row:tap_row + map_side, tap_col:tap_col + map_side, :]  43 us
    psum x1, waiting for transfers between devices, shards(): lax.psum(shares[3].astype(jnp.bfloat16), 'img').astype(jnp.float32)  42.2 us
    dot_general x8, matrix products, dense(): return jnp.dot(left_op, right_op, preferred_element_type=jnp.float32)  41.9 us
  transfers between devices with their start and end apart: 22, of which 13 were waited for; matrix products, arithmetic and copies ran while one was open for 32% of the time, Pallas kernels for 0%

commit v1 on v0

v1 whole, which is shorter than its diff:
```python
import functools

import jax
import jax.numpy as jnp
from jax import lax
from jax.experimental import pallas as pl
from jax.experimental.pallas import tpu as pltpu
from jax.sharding import PartitionSpec as P

F32 = jnp.float32
BF16 = jnp.bfloat16
HEAD_DIM = 32
WIN = 7
COLS = 8
TOK = WIN * COLS
WPC = 4
LINES = WPC * WIN
CHUNK = WPC * TOK
LANES = 128
EPSILON = 1e-05
MASK_FILL = 1000000000.0
VMEM = 56 * 1024 * 1024
GRP = ("line", "core")


def nn(a, b):
    return lax.dot_general(a, b, (((1,), (0,)), ((), ())), preferred_element_type=F32)


def nt(a, b):
    return lax.dot_general(a, b, (((1,), (1,)), ((), ())), preferred_element_type=F32)


def tn(a, b):
    return lax.dot_general(a, b, (((0,), (0,)), ((), ())), preferred_element_type=F32)


def channel_scale():
    return (14 * WIN * WIN) ** (-0.5)


def lane_slices(width):
    return [slice(s, s + LANES) for s in range(0, width, LANES)]


def head_mask(rows, head, dtype):
    lane = lax.broadcasted_iota(jnp.int32, (rows, LANES), 1)
    return jnp.where(lane // HEAD_DIM == head, 1.0, 0.0).astype(dtype)


def block_mask(dtype):
    row = lax.broadcasted_iota(jnp.int32, (LANES, LANES), 0)
    lane = lax.broadcasted_iota(jnp.int32, (LANES, LANES), 1)
    return jnp.where(row // HEAD_DIM == lane // HEAD_DIM, 1.0, 0.0).astype(dtype)


class Where:
    def __init__(self, globs, chunk, place, glob_image, loc_image, extent):
        self.globs, self.chunk, self.place = globs, chunk, place
        self.glob_image, self.loc_image, self.extent = glob_image, loc_image, extent
        self.is_glob = chunk < globs
        self.local = jnp.maximum(chunk - globs, 0) * WPC
        self.gate = jnp.where(self.is_glob, 1.0, 0.0)

    def sides(self, w):
        return [
            jnp.where(self.is_glob, WIN, self.extent[side, self.local + w]) for side in range(2)
        ]

    def image(self, w, images):
        core, line, lines_of = self.place[0], self.place[1], self.place[3]
        me = line * 2 + core
        locs = self.extent.shape[1]
        image = jnp.where(
            self.is_glob,
            self.glob_image[me * self.globs + jnp.minimum(self.chunk, self.globs - 1)],
            self.loc_image[me * locs + self.local + w],
        )
        per = images // (2 * lines_of)
        owner = image // per
        side = jnp.bitwise_xor(owner % 2, core) * lines_of
        return (side + jnp.bitwise_xor(owner // 2, line)) * per + image % per


def fill_valid(where, valid):
    for w in range(WPC):
        row = lax.broadcasted_iota(jnp.int32, (WIN, COLS, LANES), 0)
        col = lax.broadcasted_iota(jnp.int32, (WIN, COLS, LANES), 1)
        high, wide = where.sides(w)
        inside = (row < high) & (col < wide)
        valid[WIN * w : WIN * w + WIN] = jnp.where(inside, 1.0, 0.0)


def fill_vec(kernels, gains, shifts, vec):
    for t in range(9):
        both = kernels[t].astype(F32)
        vec[t : t + 1] = both[0:1]
        vec[9 + t : 10 + t] = both[1:2]
    vec[18:20] = gains[...].astype(F32)
    vec[20 : 20 + shifts.shape[0]] = shifts[...].astype(F32)


def load_tokens(chunk, globs, glob_ref, loc_ref, dst, wide):
    @pl.when(chunk < globs)
    def _():
        wide[:, 0:14, :] = glob_ref[0].astype(F32)
        for w in range(WPC):
            a, b = divmod(w, 2)
            tile = wide[WIN * a : WIN * a + WIN, pl.ds(WIN * b, COLS), :]
            col = lax.broadcasted_iota(jnp.int32, tile.shape, 1)
            dst[WIN * w : WIN * w + WIN] = jnp.where(col < WIN, tile, 0.0)

    @pl.when(chunk >= globs)
    def _():
        for w in range(WPC):
            dst[WIN * w : WIN * w + WIN, 0:WIN, :] = loc_ref[w].astype(F32)
        dst[:, WIN:COLS, :] = jnp.zeros((LINES, 1, dst.shape[2]), F32)


def store_tokens(chunk, globs, src, glob_ref, loc_ref, wide):
    @pl.when(chunk < globs)
    def _():
        for b in range(2):
            for a in range(2):
                w = 2 * a + b
                wide[WIN * a : WIN * a + WIN, pl.ds(WIN * b, COLS), :] = src[
                    WIN * w : WIN * w + WIN
                ]
        glob_ref[0] = wide[:, 0:14, :].astype(glob_ref.dtype)

    @pl.when(chunk >= globs)
    def _():
        for w in range(WPC):
            loc_ref[w] = src[WIN * w : WIN * w + WIN, 0:WIN, :].astype(loc_ref.dtype)


def shifted(tiles, gate):
    left = [pltpu.roll(t, 1, 1) for t in tiles]
    right = [pltpu.roll(t, COLS - 1, 1) for t in tiles]
    col = lax.broadcasted_iota(jnp.int32, tiles[0].shape, 1)
    for w in (1, 3):
        left[w] = jnp.where(col == 0, gate * pltpu.roll(left[w - 1], 1, 1), left[w])
    for w in (0, 2):
        right[w] = jnp.where(
            col == WIN - 1, gate * pltpu.roll(right[w + 1], COLS - 1, 1), right[w]
        )
    none = jnp.zeros((1, COLS, LANES), F32)
    result = []
    for kind in (left, tiles, right):
        result.append(
            [
                jnp.concatenate(
                    [
                        gate * kind[w - 2][WIN - 1 : WIN] if w >= 2 else none,
                        kind[w],
                        gate * kind[w + 2][0:1] if w < 2 else none,
                    ],
                    axis=0,
                )
                for w in range(WPC)
            ]
        )
    return result


def row_of(vec, row, lanes):
    return vec[row : row + 1, lanes].reshape(1, 1, LANES)


def conv_forward(src, valid, vec, kernel_row, bias_row, gate, dst):
    for lanes in lane_slices(src.shape[2]):
        tiles = [src[WIN * w : WIN * w + WIN, :, lanes] for w in range(WPC)]
        masked = [tiles[w] * valid[WIN * w : WIN * w + WIN] for w in range(WPC)]
        kinds = shifted(masked, gate)
        taps = [row_of(vec, kernel_row + t, lanes) for t in range(9)]
        bias = row_of(vec, bias_row, lanes)
        for w in range(WPC):
            total = tiles[w] + bias
            for i in range(3):
                for j in range(3):
                    total = total + kinds[j][w][i : i + WIN] * taps[3 * i + j]
            dst[WIN * w : WIN * w + WIN, :, lanes] = total


def conv_backward(grad, src, valid, vec, kernel_row, gate, dst, acc, acc_row, acc_bias_row):
    for lanes in lane_slices(src.shape[2]):
        tiles = [grad[WIN * w : WIN * w + WIN, :, lanes] for w in range(WPC)]
        kinds = shifted(tiles, gate)
        taps = [row_of(vec, kernel_row + t, lanes) for t in range(9)]
        sums = [None] * 9
        bias_sum = None
        for w in range(WPC):
            mask = valid[WIN * w : WIN * w + WIN]
            masked = src[WIN * w : WIN * w + WIN, :, lanes] * mask
            total = None
            for i in range(3):
                for j in range(3):
                    piece = kinds[2 - j][w][2 - i : 2 - i + WIN]
                    term = piece * taps[3 * i + j]
                    total = term if total is None else total + term
                    part = jnp.sum(piece * masked, axis=0)
                    t = 3 * i + j
                    sums[t] = part if sums[t] is None else sums[t] + part
            dst[WIN * w : WIN * w + WIN, :, lanes] = tiles[w] + total * mask
            part = jnp.sum(tiles[w], axis=0)
            bias_sum = part if bias_sum is None else bias_sum + part
        for t in range(9):
            acc[acc_row + t, :, lanes] += sums[t]
        acc[acc_bias_row, :, lanes] += bias_sum


def norm_blocks(src):
    width = src.shape[2]

    def block(b):
        return src[b : b + 4].reshape(4 * COLS, width)

    starts = range(0, LINES, 4)
    means = [jnp.mean(block(b), axis=-1, keepdims=True) for b in starts]
    spreads = []
    for b, mean in zip(starts, means):
        x = block(b) - mean
        spreads.append(jnp.mean(x * x, axis=-1, keepdims=True))
    scales = [lax.rsqrt(v + EPSILON) for v in spreads]
    return starts, block, means, scales


def norm_forward(src, vec, gain_row, shift_row, dst):
    gain = vec[gain_row : gain_row + 1, :]
    shift = vec[shift_row : shift_row + 1, :]
    starts, block, means, scales = norm_blocks(src)
    for b, mean, scale in zip(starts, means, scales):
        x = (block(b) - mean) * scale
        dst[b * COLS : (b + 4) * COLS, :] = (x * gain + shift).astype(BF16)


def norm_backward(grad, src, vec, gain_row, base, dst, acc, acc_gain, acc_shift):
    gain = vec[gain_row : gain_row + 1, :]
    width = src.shape[2]
    gain_sum = jnp.zeros((COLS, width), F32)
    shift_sum = jnp.zeros((COLS, width), F32)
    starts, block, means, scales = norm_blocks(src)
    sums = []
    for b, mean, scale in zip(starts, means, scales):
        x = (block(b) - mean) * scale
        g = grad[b * COLS : (b + 4) * COLS, :]
        gx = g * x
        gain_sum = gain_sum + jnp.sum(gx.reshape(4, COLS, width), axis=0)
        shift_sum = shift_sum + jnp.sum(g.reshape(4, COLS, width), axis=0)
        sums.append(
            (
                jnp.mean(g * gain, axis=-1, keepdims=True),
                jnp.mean(gx * gain, axis=-1, keepdims=True),
            )
        )
    for b, mean, scale, (mean_g, mean_gx) in zip(starts, means, scales, sums):
        x = (block(b) - mean) * scale
        g = grad[b * COLS : (b + 4) * COLS, :] * gain
        result = (g - mean_g - x * mean_gx) * scale
        dst[b : b + 4] = base[b : b + 4] + result.reshape(4, COLS, width)
    acc[acc_gain] += gain_sum
    acc[acc_shift] += shift_sum


def gelu_parts(u):
    phi = 0.5 + 0.5 * lax.erf(u * 0.7071067811865476)
    return u * phi, phi + u * (0.3989422804014327 * jnp.exp(-0.5 * u * u))


def column_sums(value, rows=CHUNK):
    return jnp.sum(value.reshape(rows // COLS, COLS, value.shape[1]), axis=0)


def feed_forward(h, w1, b1, act, slope):
    width = 512
    hidden = h[...]
    for s in range(0, w1.shape[1], width):
        u = nn(hidden, w1[:, s : s + width]) + b1[:, s : s + width].astype(F32)
        for r in range(0, CHUNK, 32):
            for c in range(0, width, 256):
                value, deriv = gelu_parts(u[r : r + 32, c : c + 256])
                act[r : r + 32, s + c : s + c + 256] = value.astype(BF16)
                slope[r : r + 32, s + c : s + c + 256] = deriv.astype(slope.dtype)


def feed_backward(product, slope, du, acc_bias):
    width = 512
    for s in range(0, slope.shape[1], width):
        dg = product(s, s + width).astype(F32)
        for c in range(0, width, 256):
            total = jnp.zeros((COLS, 256), F32)
            for r in range(0, CHUNK, 32):
                value = (
                    dg[r : r + 32, c : c + 256]
                    * slope[r : r + 32, s + c : s + c + 256].astype(F32)
                ).astype(BF16)
                du[r : r + 32, s + c : s + c + 256] = value
                total = total + column_sums(value.astype(F32), 32)
            acc_bias[:, s + c : s + c + 256] += total


def stretched(value):
    empty = jnp.zeros((COLS, value.shape[1]), F32)
    return jnp.concatenate([value, empty], axis=0).astype(BF16)


def by_head(value):
    return jnp.concatenate(
        [value * head_mask(value.shape[0], h, BF16) for h in range(LANES // HEAD_DIM)], axis=0
    )


def own_heads(product):
    size = COLS * COLS
    return sum(
        product[h * size : h * size + TOK, :] * head_mask(TOK, h, F32)
        for h in range(LANES // HEAD_DIM)
    )


def key_bias(where, window):
    size = COLS * COLS
    row = lax.broadcasted_iota(jnp.int32, (size, LANES), 0)
    high, wide = where.sides(window)
    inside = (row // COLS < high) & (row % COLS < wide)
    one = jnp.where(inside, 0.0, -MASK_FILL)
    return jnp.concatenate([one, one], axis=1)


def window_probs(keys, by_query, bias):
    scores = nt(keys, by_query) * HEAD_DIM ** (-0.5) + bias
    exponent = jnp.exp(scores - jnp.max(scores, axis=0, keepdims=True))
    return exponent * (1.0 / jnp.sum(exponent, axis=0, keepdims=True))


def window_rows(w):
    if isinstance(w, int):
        return slice(w * TOK, (w + 1) * TOK)
    return pl.ds(pl.multiple_of(w * TOK, COLS), TOK)


def spatial_forward(where, proj, dst, kept):
    width = dst.shape[1]

    def one(w):
        rows = window_rows(w)
        bias = key_bias(where, w)
        for k, s in enumerate(range(0, width, LANES)):
            query = stretched(proj[rows, s : s + LANES])
            keys = stretched(proj[rows, width + s : width + s + LANES])
            values = stretched(proj[rows, 2 * width + s : 2 * width + s + LANES])
            probs = window_probs(keys, by_head(query), bias)
            kept[w, k] = probs
            dst[rows, s : s + LANES] = own_heads(tn(probs.astype(BF16), values))

    for w in range(WPC):
        one(w)


def spatial_backward(kept, proj, upstream, dst):
    width = upstream.shape[1]
    scale = HEAD_DIM ** (-0.5)
    starts = range(0, width, LANES)
    for w in range(WPC):
        rows = window_rows(w)
        grads = [by_head(stretched(upstream[rows, s : s + LANES])) for s in starts]
        dprobs = []
        for s, grad in zip(starts, grads):
            values = stretched(proj[rows, 2 * width + s : 2 * width + s + LANES])
            dprobs.append(nt(values, grad))
        dots = [jnp.sum(kept[w, k] * v, axis=0, keepdims=True) for k, v in enumerate(dprobs)]
        dscores = [
            (kept[w, k] * (v - dot)).astype(BF16) for k, (v, dot) in enumerate(zip(dprobs, dots))
        ]
        for k, s in enumerate(starts):
            v_s = slice(2 * width + s, 2 * width + s + LANES)
            dst[rows, v_s] = nn(kept[w, k].astype(BF16), grads[k])[0:TOK]
        for k, s in enumerate(starts):
            query = by_head(stretched(proj[rows, s : s + LANES]))
            keys = stretched(proj[rows, width + s : width + s + LANES])
            dst[rows, s : s + LANES] = own_heads(tn(dscores[k], keys)) * scale
            k_s = slice(width + s, width + s + LANES)
            dst[rows, k_s] = nn(dscores[k], query)[0:TOK] * scale


def by_window(value):
    row = lax.broadcasted_iota(jnp.int32, value.shape, 0)
    return jnp.concatenate(
        [
            value * jnp.where((row >= w * TOK) & (row < (w + 1) * TOK), 1.0, 0.0).astype(BF16)
            for w in range(WPC)
        ],
        axis=1,
    )


def own_windows(product):
    return jnp.concatenate(
        [
            product[w * TOK : (w + 1) * TOK, w * LANES : (w + 1) * LANES] for w in range(WPC)
        ],
        axis=0,
    )


def gram_add(where, left, right, acc):
    images = [where.image(w, acc.shape[0]) for w in range(WPC)]
    for s in range(0, acc.shape[2], LANES):
        full = tn(left(s), by_window(right(s)))
        for w in range(WPC):
            part = sum(
                full[h * HEAD_DIM : (h + 1) * HEAD_DIM, w * LANES : (w + 1) * LANES]
                * head_mask(HEAD_DIM, h, F32)
                for h in range(LANES // HEAD_DIM)
            )
            acc[images[w], :, s : s + LANES] += part


def image_blocks(table, images, s, axis):
    return jnp.concatenate([head_blocks(table[i, :, s : s + LANES]) for i in images], axis=axis)


def gram_out(chunk, acc, mine, other):
    half = acc.shape[0] // 2

    @pl.when(chunk == pl.num_programs(0) - 1)
    def _():
        mine[...] = acc[0:half].reshape(mine.shape)
        other[...] = acc[half : 2 * half].reshape(other.shape)


def vector_out(chunk, acc, vec, bias_acc=None, bias=None):
    @pl.when(chunk == pl.num_programs(0) - 1)
    def _():
        vec[...] = jnp.sum(acc[...], axis=1)
        if bias is not None:
            bias[...] = jnp.sum(bias_acc[...], axis=0, keepdims=True)


def head_blocks(packed):
    return jnp.concatenate([packed] * (LANES // HEAD_DIM), axis=0) * block_mask(BF16)


def as_lines(value):
    return value.reshape(LINES, COLS, value.shape[1])


def spatial_kernel(
    globs, place, gi, li, ext,
    gx, lx, sk, sg, ss, ck, cg, cs, sb1, wqkv, wproj, w1, w2, wcqkv,
    c1_o, h1_o, p_o, o_o, c2_o, c3_o, h2_o, g_o, gp_o, mid_o, cc1_o, ch1_o, cp_o, probs_o,
    mine_o, other_o,
    wide, tok, valid, proj, att, gram, sv, cv,
):
    chunk = pl.program_id(0)
    width = gx.shape[3]
    where = Where(globs, chunk, place, gi, li, ext)
    gate = where.gate

    @pl.when(chunk == 0)
    def _():
        gram[...] = jnp.zeros_like(gram)
        wide[:, 14:16, :] = jnp.zeros((14, 2, width), F32)
        fill_vec(sk, sg, ss, sv)
        fill_vec(ck, cg, cs, cv)

    fill_valid(where, valid)
    load_tokens(chunk, globs, gx, lx, tok, wide)
    conv_forward(tok, valid, sv, 0, 20, gate, c1_o)
    norm_forward(c1_o, sv, 18, 22, h1_o)
    for j in range(3):
        cols = slice(j * width, (j + 1) * width)
        part = nn(h1_o[...], wqkv[:, cols])
        if j != 1:
            row = 24 if j == 0 else 25
            part = part + sv[row : row + 1, :]
        part = part.astype(BF16)
        p_o[:, cols] = part
        proj[:, cols] = part.astype(F32)
    spatial_forward(where, proj, att, probs_o)
    o_o[...] = att[...].astype(BF16)
    c2_o[...] = c1_o[...] + as_lines(nn(o_o[...], wproj[...]) + sv[26:27, :])
    conv_forward(c2_o, valid, sv, 9, 21, gate, c3_o)
    norm_forward(c3_o, sv, 19, 23, h2_o)
    feed_forward(h2_o, w1, sb1, g_o, gp_o)
    mid_o[...] = c3_o[...] + as_lines(nn(g_o[...], w2[...]) + sv[27:28, :])
    conv_forward(mid_o, valid, cv, 0, 20, gate, cc1_o)
    norm_forward(cc1_o, cv, 18, 22, ch1_o)
    for j in range(3):
        cols = slice(j * width, (j + 1) * width)
        part = nn(ch1_o[...], wcqkv[:, cols]) + cv[24 + j : 25 + j, :]
        if j == 0:
            mask = jnp.concatenate([valid[...].reshape(CHUNK, LANES)] * (width // LANES), axis=1)
            part = part * mask
        cp_o[:, cols] = part.astype(BF16)
    gram_add(
        where,
        lambda s: cp_o[:, width + s : width + s + LANES],
        lambda s: cp_o[:, s : s + LANES],
        gram,
    )
    gram_out(chunk, gram, mine_o, other_o)


def channel_kernel(
    globs, place, gi, li, ext,
    a_all, cc1, cvals, dout, dg, vec_i, ck, cg, cs, cb1, wproj, w1, w1_t, w2,
    gout, lout, o_o, h2_o, g_o, du_o, dc2_o, dob_o, do_o, mine_o, other_o, vec_o, bias_o,
    wide, tok, valid, c2_s, c3_s, slope, dhid, dgram, vg, vb, cv,
):
    chunk = pl.program_id(0)
    width = cc1.shape[2]
    where = Where(globs, chunk, place, gi, li, ext)
    gate = where.gate

    @pl.when(chunk == 0)
    def _():
        dgram[...] = jnp.zeros_like(dgram)
        vg[...] = jnp.zeros_like(vg)
        vb[...] = jnp.zeros_like(vb)
        wide[:, 14:16, :] = jnp.zeros((14, 2, width), F32)
        fill_vec(ck, cg, cs, cv)
        vg[:, 0, :] = vec_i[...]

    fill_valid(where, valid)
    images = [where.image(w, a_all.shape[0]) for w in range(WPC)]
    for s in range(0, width, LANES):
        product = nn(cvals[:, s : s + LANES], image_blocks(a_all, images, s, 1))
        o_o[:, s : s + LANES] = own_windows(product).astype(BF16)
    c2_s[...] = cc1[...] + as_lines(nn(o_o[...], wproj[...]) + cv[27:28, :])
    conv_forward(c2_s, valid, cv, 9, 21, gate, c3_s)
    norm_forward(c3_s, cv, 19, 23, h2_o)
    feed_forward(h2_o, w1, cb1, g_o, slope)
    tok[...] = c3_s[...] + as_lines(nn(g_o[...], w2[...]) + cv[28:29, :])
    store_tokens(chunk, globs, tok, gout, lout, wide)

    tok[...] = as_lines(dout[...].astype(F32))
    feed_backward(lambda s, e: dg[:, s:e], slope, du_o, vb)
    dhid[...] = nn(du_o[...], w1_t[...])
    norm_backward(dhid, c3_s, cv, 19, tok, tok, vg, 10, 11)
    conv_backward(tok, c2_s, valid, cv, 9, gate, dc2_o, vg, 0, 9)
    low = dc2_o[...].reshape(CHUNK, width).astype(BF16)
    dob_o[...] = low
    vg[12] += column_sums(low.astype(F32))
    do_o[...] = nt(dob_o[...], wproj[...]).astype(BF16)
    gram_add(
        where,
        lambda s: cvals[:, s : s + LANES],
        lambda s: do_o[:, s : s + LANES],
        dgram,
    )
    gram_out(chunk, dgram, mine_o, other_o)
    vector_out(chunk, vg, vec_o, vb, bias_o)


def channel_back_kernel(
    globs, place, gi, li, ext,
    a_all, ds_all, cp, do, dc2, cc1, mid, ck, cg, cs, wqkv,
    dp_o, dmid_o, vec_o,
    tok, valid, dhid, vg, cv,
):
    chunk = pl.program_id(0)
    width = do.shape[1]
    where = Where(globs, chunk, place, gi, li, ext)
    gate = where.gate

    @pl.when(chunk == 0)
    def _():
        vg[...] = jnp.zeros_like(vg)
        fill_vec(ck, cg, cs, cv)

    fill_valid(where, valid)
    scale = channel_scale()
    images = [where.image(w, a_all.shape[0]) for w in range(WPC)]
    mask = valid[...].reshape(CHUNK, LANES)
    for s in range(0, width, LANES):
        q_s, k_s, v_s = [slice(j * width + s, j * width + s + LANES) for j in range(3)]
        blocks = image_blocks(ds_all, images, s, 1)
        low = (own_windows(nn(cp[:, k_s], blocks)) * (scale * mask)).astype(BF16)
        dp_o[:, q_s] = low
        vg[12, :, s : s + LANES] += column_sums(low.astype(F32))
        blocks = image_blocks(ds_all, images, s, 0)
        low = (own_windows(nt(cp[:, q_s], blocks)) * scale).astype(BF16)
        dp_o[:, k_s] = low
        vg[13, :, s : s + LANES] += column_sums(low.astype(F32))
        blocks = image_blocks(a_all, images, s, 0)
        low = own_windows(nt(do[:, s : s + LANES], blocks)).astype(BF16)
        dp_o[:, v_s] = low
        vg[14, :, s : s + LANES] += column_sums(low.astype(F32))
    dhid[...] = nt(dp_o[...], wqkv[...])
    norm_backward(dhid, cc1, cv, 18, dc2, tok, vg, 10, 11)
    conv_backward(tok, mid, valid, cv, 0, gate, dmid_o, vg, 0, 9)
    vector_out(chunk, vg, vec_o)


def cot_kernel(globs, place, gcot, lcot, w2, dout_o, dg_o, vec_o, wide, tok, vg):
    chunk = pl.program_id(0)
    width = gcot.shape[3]

    @pl.when(chunk == 0)
    def _():
        vg[...] = jnp.zeros_like(vg)
        wide[:, 14:16, :] = jnp.zeros((14, 2, width), F32)

    load_tokens(chunk, globs, gcot, lcot, tok, wide)
    flat = tok[...].reshape(CHUNK, width)
    vg[13] += column_sums(flat)
    dout_o[...] = flat.astype(BF16)
    for s in range(0, w2.shape[0], 512):
        dg_o[:, s : s + 512] = nt(dout_o[...], w2[s : s + 512, :]).astype(BF16)
    vector_out(chunk, vg, vec_o)


def turn_kernel(*refs):
    half = len(refs) // 2
    for src, dst in zip(refs[:half], refs[half:]):
        dst[...] = jnp.transpose(src[...])


def turned_weights(*weights):
    steps = 4

    def spec(shape, step_dim):
        block = tuple(n // steps if d == step_dim else n for d, n in enumerate(shape))
        return pl.BlockSpec(block, lambda j: (j, 0) if step_dim == 0 else (0, j))

    longs = [0 if w.shape[0] > w.shape[1] else 1 for w in weights]
    return pl.pallas_call(
        turn_kernel,
        grid=(steps,),
        in_specs=[spec(w.shape, d) for w, d in zip(weights, longs)],
        out_specs=[spec(w.shape[::-1], 1 - d) for w, d in zip(weights, longs)],
        out_shape=[jax.ShapeDtypeStruct(w.shape[::-1], BF16) for w in weights],
        compiler_params=pltpu.CompilerParams(
            dimension_semantics=("arbitrary",), vmem_limit_bytes=VMEM
        ),
        name="turned_weights",
    )(*weights)


def hidden_back_kernel(
    globs, place, gi, li, ext,
    c2, c3, gp, dmid, sk, sg, ss, wproj, w1_t, w2_t,
    du_o, dmb_o, dob_o, dc2_o, do_o, vec_o, bias_o,
    tok, valid, dhid, vg, vb, sv,
):
    chunk = pl.program_id(0)
    width = wproj.shape[0]
    where = Where(globs, chunk, place, gi, li, ext)

    @pl.when(chunk == 0)
    def _():
        vg[...] = jnp.zeros_like(vg)
        vb[...] = jnp.zeros_like(vb)
        fill_vec(sk, sg, ss, sv)

    fill_valid(where, valid)
    low = dmid[...].reshape(CHUNK, width).astype(BF16)
    dmb_o[...] = low
    vg[13] += column_sums(low.astype(F32))
    upstream = dmb_o[...]
    feed_backward(lambda s, e: nn(upstream, w2_t[:, s:e]), gp, du_o, vb)
    dhid[...] = nn(du_o[...], w1_t[...])
    norm_backward(dhid, c3, sv, 19, dmid, tok, vg, 10, 11)
    conv_backward(tok, c2, valid, sv, 9, where.gate, dc2_o, vg, 0, 9)
    low = dc2_o[...].reshape(CHUNK, width).astype(BF16)
    dob_o[...] = low
    vg[12] += column_sums(low.astype(F32))
    do_o[...] = nt(dob_o[...], wproj[...]).astype(BF16)
    vector_out(chunk, vg, vec_o, vb, bias_o)


def window_back_kernel(probs, p, do, *refs):
    dp_o, vec_o, proj, att, dproj, vg = refs[-6:]
    chunk = pl.program_id(0)
    width = do.shape[1]

    @pl.when(chunk == 0)
    def _():
        vg[...] = jnp.zeros_like(vg)
        if len(refs) > 6:
            vg[:, 0, :] = refs[0][...]

    att[...] = do[...].astype(F32)
    proj[...] = p[...].astype(F32)
    spatial_backward(probs, proj, att, dproj)
    for j in range(3):
        low = dproj[:, j * width : (j + 1) * width].astype(BF16)
        dp_o[:, j * width : (j + 1) * width] = low
        vg[12 + j] += column_sums(low.astype(F32))
    vector_out(chunk, vg, vec_o)


def window_back(probs, p, do, first, count, base):
    width = do.shape[1]
    specs = [
        pl.BlockSpec((WPC,) + probs.shape[1:], lambda i: (i + first, 0, 0, 0)),
        pl.BlockSpec((CHUNK, 3 * width), lambda i: (i + first, 0)),
        pl.BlockSpec((CHUNK, width), lambda i: (i + first, 0)),
    ]
    args, aliases = [probs, p, do], {}
    if base is not None:
        args += [base[1], base[0]]
        specs += [keep((16, width)), pl.BlockSpec(memory_space=pl.ANY)]
        aliases = {4: 0}
    return pl.pallas_call(
        window_back_kernel,
        grid=(count,),
        in_specs=specs,
        out_specs=[
            pl.BlockSpec((CHUNK, 3 * width), lambda i: (i + first, 0)),
            keep((16, width)),
        ],
        out_shape=[
            jax.ShapeDtypeStruct(p.shape, BF16),
            jax.ShapeDtypeStruct((16, width), F32),
        ],
        scratch_shapes=[
            pltpu.VMEM((CHUNK, 3 * width), F32),
            pltpu.VMEM((CHUNK, width), F32),
            pltpu.VMEM((CHUNK, 3 * width), F32),
            pltpu.VMEM((16, COLS, width), F32),
        ],
        input_output_aliases=aliases,
        compiler_params=pltpu.CompilerParams(
            dimension_semantics=("arbitrary",), vmem_limit_bytes=VMEM
        ),
        cost_estimate=pl.CostEstimate(
            flops=16 * count * CHUNK * 256 * width,
            bytes_accessed=count * (16 * CHUNK * width + 4 * probs[0].size * WPC),
            transcendentals=0,
        ),
        name="window_back",
    )(*args)


def first_back_kernel(
    globs, place, gi, li, ext,
    gx, lx, c1, dp, dc2, sk, sg, ss, wqkv, vec_i,
    gg, lg, vec_o,
    wide, tok, tok2, valid, dhid, vg, sv,
):
    chunk = pl.program_id(0)
    width = gx.shape[3]
    where = Where(globs, chunk, place, gi, li, ext)

    @pl.when(chunk == 0)
    def _():
        vg[...] = jnp.zeros_like(vg)
        vg[:, 0, :] = vec_i[...]
        wide[:, 14:16, :] = jnp.zeros((14, 2, width), F32)
        fill_vec(sk, sg, ss, sv)

    fill_valid(where, valid)
    dhid[...] = nt(dp[...], wqkv[...])
    norm_backward(dhid, c1, sv, 18, dc2, tok2, vg, 10, 11)
    load_tokens(chunk, globs, gx, lx, tok, wide)
    lines_ref = dhid.reshape(LINES, COLS, width)
    conv_backward(tok2, tok, valid, sv, 0, where.gate, lines_ref, vg, 0, 9)
    store_tokens(chunk, globs, lines_ref, gg, lg, wide)
    vector_out(chunk, vg, vec_o)


def weight_kernel(y, x, out):
    out[...] = tn(y[...], x[...]).astype(BF16).reshape(out.shape)


def group_kernel(kinds, counts, mode, skip, place, *refs):
    ins = sum(counts)
    outs = 1 if mode == "one" else 2
    static = mode != "xor"
    buffers, product = refs[ins + skip : ins + skip + outs], refs[ins + skip + outs]
    turned = list(refs[ins + skip + outs + 1 :])
    shape = buffers[0].shape
    parts, lines_of, lanes = shape[-4], shape[-3], shape[-1]
    core, line, quarter = (0, 0, 0) if static else (place[0], place[1], place[2])
    step = pl.program_id(0)

    def put(q, j, at, values, lane=0):
        rows = slice(at, at + values[0].shape[0])
        cols = slice(lane, lane + values[0].shape[1])
        if mode == "pair":
            swap = place[0] == 1
            values = [jnp.where(swap, values[1 - rel], values[rel]) for rel in range(2)]
            q = jnp.bitwise_xor(place[2], q)
        for rel in range(2):
            value = values[rel].astype(BF16)
            if mode == "one":
                buffers[0][rel, q, j, rows, cols] = value
            else:
                buffers[rel][q, j, rows, cols] = value

    def rows_at(start, size):
        if isinstance(start, int):
            return slice(start, start + size)
        return pl.ds(pl.multiple_of(start, 16), size)

    at, first = 0, 0
    for kind, count in zip(kinds, counts):
        args = refs[first : first + count]
        first += count
        if kind == "vec":
            *vecs, bias_a, bias_b = args
            col = vecs[0].shape[1] // (2 * lines_of)
            size = bias_a.shape[1] // (2 * lines_of)

            @pl.when(step == 0)
            def _(vecs=vecs, bias_a=bias_a, bias_b=bias_b, at=at, col=col, size=size):
                cuts = [slice(k * col, (k + 1) * col) for k in range(2 * lines_of)]
                wide = [slice(k * size, (k + 1) * size) for k in range(2 * lines_of)]
                fill = jnp.zeros((14, size), F32)
                for j in range(lines_of):
                    for q, vec in enumerate(vecs):
                        put(q, j, at, [vec[:, cuts[2 * j + rel]] for rel in range(2)])
                    last = [
                        jnp.concatenate(
                            [bias_a[:, wide[2 * j + rel]], bias_b[:, wide[2 * j + rel]], fill],
                            axis=0,
                        )
                        for rel in range(2)
                    ]
                    put(parts - 1, j, at, last)

            at += 16
        elif kind == "side":
            y, x = args
            x_t = turned.pop(0)

            @pl.when(step == 0)
            def _(x=x, x_t=x_t):
                x_t[...] = jnp.transpose(x[...])

            size = y.shape[1] // 2
            halves = [nn(x_t[...], y[:, rel * size : (rel + 1) * size]) for rel in range(2)]
            each = size // parts
            for q in range(parts):
                for half in range(lanes // size):
                    start = (q * (lanes // size) + half) * each
                    values = [halves[rel][start : start + each, :] for rel in range(2)]
                    put(q, step, at, values, half * size)
            at += each
        else:
            y, x = args
            n = y.shape[1]
            if kind == "rows":
                y_t = turned.pop(0)

                @pl.when(step == 0)
                def _(y=y, y_t=y_t):
                    y_t[...] = jnp.transpose(y[...])

                result = nn(y_t[...], x[...])
                each = n // (2 * lines_of)
            else:
                result = tn(y[...], x[...])
                each = n // (2 * parts)
            if not static:
                product[0:n, :] = result
                result = product
            for e in range(lines_of if kind == "rows" else parts):
                values = []
                for rel in range(2):
                    side = core ^ rel if static else jnp.bitwise_xor(core, rel)
                    mine = line if kind == "rows" else quarter
                    own = mine ^ e if static else jnp.bitwise_xor(mine, e)
                    if kind == "rows":
                        start = (own * 2 + side) * each
                    else:
                        start = (side * parts + own) * each
                    values.append(result[rows_at(start, each), :])
                if kind == "rows":
                    put(step, e, at, values)
                else:
                    put(e, step, at, values)
            at += each


def group_grad(
    place, groups, kinds, mode, lanes, lines_of, parts, name, blocks=(0, 1), base=None, hint=1
):
    total = groups[0][0].shape[0]
    specs, args, rows, flops, turned = [], [], 0, 0, []

    def moving(size, which):
        if mode != "xor":
            return pl.BlockSpec((total, size), lambda j, at: (0, j))
        return pl.BlockSpec((total, size), lambda j, at: (0, jnp.bitwise_xor(at[which], j)))

    for operands, kind in zip(groups, kinds):
        args += operands
        if kind == "vec":
            specs += [keep(v.shape) for v in operands]
            rows += 16
            continue
        y, x = operands
        n, m = y.shape[1], x.shape[1]
        flops += 2 * total * n * m
        if kind == "rows":
            specs += [hold((total, n)), moving(m // parts, 2)]
            turned.append(pltpu.VMEM((n, total), BF16))
            rows += n // (2 * lines_of)
        else:
            specs += [moving(n // lines_of, 1), hold((total, m))]
            if kind == "side":
                turned.append(pltpu.VMEM((m, total), BF16))
            rows += n * m // (2 * lines_of * parts * lanes)
    block, count = blocks
    if mode == "one":
        outs = [jax.ShapeDtypeStruct((2, parts, lines_of, count * rows, lanes), BF16)]
        out_specs = [
            pl.BlockSpec((2, parts, lines_of, rows, lanes), lambda j, at: (0, 0, 0, block, 0))
        ]
    else:
        outs = [jax.ShapeDtypeStruct((parts, lines_of, rows, lanes), BF16)] * 2
        out_specs = [keep(o.shape) for o in outs]
    aliases = {}
    if base is not None:
        aliases = {1 + len(args): 0}
        args.append(base)
        specs.append(pl.BlockSpec(memory_space=pl.ANY))
    size = sum(a.size * a.dtype.itemsize for a in args) + 4 * parts * lines_of * rows * lanes
    counts = [len(g) for g in groups]
    return pl.pallas_call(
        functools.partial(group_kernel, kinds, counts, mode, 0 if base is None else 1),
        grid_spec=pltpu.PrefetchScalarGridSpec(
            num_scalar_prefetch=1,
            grid=(parts,),
            in_specs=specs,
            out_specs=out_specs,
            scratch_shapes=[pltpu.VMEM((512, lanes), F32)] + turned,
        ),
        out_shape=outs,
        input_output_aliases=aliases,
        compiler_params=pltpu.CompilerParams(
            dimension_semantics=("arbitrary",), vmem_limit_bytes=VMEM
        ),
        cost_estimate=pl.CostEstimate(
            flops=hint * flops, bytes_accessed=hint * size, transcendentals=0
        ),
        name=name,
    )(place, *args)


def sum_kernel(count, *refs):
    ins, outs = refs[:count], refs[count:]
    for d, dst in enumerate(outs):
        total = ins[0][d].astype(F32)
        for src in ins[1:]:
            total = total + src[d].astype(F32)
        dst[...] = total.astype(dst.dtype)


def sum_split(arrays, name):
    n, rows, lanes = arrays[0].shape
    steps = 4 if rows >= 512 else 1
    kind = jax.ShapeDtypeStruct((rows, lanes), arrays[0].dtype)
    return pl.pallas_call(
        functools.partial(sum_kernel, len(arrays)),
        grid=(steps,),
        in_specs=[pl.BlockSpec((n, rows // steps, lanes), lambda j: (0, j, 0))] * len(arrays),
        out_specs=[pl.BlockSpec((rows // steps, lanes), lambda j: (j, 0))] * n,
        out_shape=[kind] * n,
        compiler_params=pltpu.CompilerParams(
            dimension_semantics=("arbitrary",), vmem_limit_bytes=VMEM
        ),
        cost_estimate=pl.CostEstimate(flops=0, bytes_accessed=0, transcendentals=0),
        name=name,
    )(*arrays)


def small_call(body, grid, args, in_specs, outs, out_specs, name):
    return pl.pallas_call(
        body,
        grid=grid,
        in_specs=in_specs,
        out_specs=out_specs,
        out_shape=outs,
        compiler_params=pltpu.CompilerParams(
            dimension_semantics=("arbitrary",), vmem_limit_bytes=VMEM
        ),
        cost_estimate=pl.CostEstimate(flops=0, bytes_accessed=0, transcendentals=0),
        name=name,
    )(*args)


def added(*refs):
    return sum(r[...].astype(F32) for r in refs)


def halved_core(mine, got):
    parts, lines_of, rows, lanes = mine.shape
    half = rows // 2
    spec = pl.BlockSpec((parts, 1, rows, lanes), lambda j: (0, j, 0, 0))
    out = jax.ShapeDtypeStruct((2, lines_of, half, lanes), BF16)
    out_spec = pl.BlockSpec((2, 1, half, lanes), lambda j: (0, j, 0, 0))
    plans = [(0, (0, 2)), (0, (1, 3)), (1, (0, 1)), (1, (2, 3))]

    def body(a, b, *outs):
        total = added(a, b).astype(BF16)
        for dst, (part, chosen) in zip(outs, plans):
            for k, q in enumerate(chosen):
                dst[k, 0] = total[q, 0, part * half : (part + 1) * half]

    return small_call(
        body, (lines_of,), (mine, got), [spec] * 2, [out] * 4, [out_spec] * 4, "s_sum_core"
    )


def halved_first(a, ra, b, rb):
    _, lines_of, half, lanes = a.shape
    spec = pl.BlockSpec((2, 1, half, lanes), lambda j: (0, j, 0, 0))
    out = jax.ShapeDtypeStruct((lines_of, half, lanes), BF16)
    out_spec = pl.BlockSpec((1, half, lanes), lambda j: (j, 0, 0))

    def body(a, ra, b, rb, a0, a1, b0, b1):
        first, second = added(a, ra).astype(BF16), added(b, rb).astype(BF16)
        a0[...], a1[...] = first[0], first[1]
        b0[...], b1[...] = second[0], second[1]

    return small_call(
        body, (lines_of,), (a, ra, b, rb), [spec] * 4, [out] * 4, [out_spec] * 4, "s_sum_first"
    )


def halved_second(a, ra, b, rb):
    lines_of, half, lanes = a.shape
    spec = pl.BlockSpec((1, half, lanes), lambda j: (j, 0, 0))
    out = jax.ShapeDtypeStruct((lines_of, 2 * half, lanes), BF16)
    out_spec = pl.BlockSpec((1, 2 * half, lanes), lambda j: (j, 0, 0))

    def body(a, ra, b, rb, dst):
        dst[:, 0:half] = added(a, ra).astype(BF16)
        dst[:, half : 2 * half] = added(b, rb).astype(BF16)

    return small_call(
        body, (lines_of,), (a, ra, b, rb), [spec] * 4, out, out_spec, "s_sum_second"
    )


def sum_with_vectors(arrays, vectors, name):
    lines_of, rows, lanes = arrays[0].shape
    extra = vectors[0].shape[0]
    out = jax.ShapeDtypeStruct((rows + extra, lanes), BF16)

    def body(*refs):
        ins, vecs = refs[: len(arrays)], refs[len(arrays) : len(arrays) + len(vectors)]
        total, vector = added(*ins).astype(BF16), added(*vecs).astype(BF16)
        for j, dst in enumerate(refs[len(arrays) + len(vectors) :]):
            dst[0:rows] = total[j]
            dst[rows : rows + extra] = vector

    return small_call(
        body, (1,), (*arrays, *vectors), [keep(v.shape) for v in (*arrays, *vectors)],
        [out] * lines_of, [keep(out.shape)] * lines_of, name,
    )


def exchange(array, axis, flip=1):
    size = lax.axis_size(axis)
    return lax.ppermute(array, axis, [(i, i ^ flip) for i in range(size)])


def group_sum_core(mine, other, name):
    parts, lines_of, rows, lanes = mine.shape
    flat = (parts, lines_of * rows, lanes)
    got = exchange(other, "core")
    return sum_split([mine.reshape(flat), got.reshape(flat)], name + "_sum_core")


def group_sum_line(pieces, name):
    held = [pieces[0]] + [exchange(pieces[d], "line", d) for d in range(1, len(pieces))]
    return sum_split([v[None] for v in held], name + "_sum_line")[0]


def quarters(mine):
    return [mine] + [exchange(mine, "img", d) for d in range(1, lax.axis_size("img"))]


def unpack_kernel(groups, place, *refs):
    ins = sum(parts for parts, _ in groups)
    pieces, outs, fulls = list(refs[:ins]), list(refs[ins : -len(groups)]), refs[-len(groups) :]
    vecs = []
    for (parts, kinds), full in zip(groups, fulls):
        for d in range(parts):
            full[jnp.bitwise_xor(place[2], d)] = pieces.pop(0)[...].astype(F32)
        at, lanes = 0, full.shape[2]
        for kind in kinds:
            if kind in ("vec", "late"):
                vecs.append((full, at))
                at += 16
                continue
            dst = outs.pop(0)
            if kind == "rows":
                rows = dst.shape[0]
                for q in range(parts):
                    dst[:, q * lanes : (q + 1) * lanes] = full[q, at : at + rows, :]
                at += rows
            elif kind == "side":
                size = dst.shape[1]
                each = size // parts
                for q in range(parts):
                    for half in range(lanes // size):
                        start = (q * (lanes // size) + half) * each
                        dst[start : start + each, :] = full[
                            q, at : at + each, half * size : (half + 1) * size
                        ]
                at += each
            else:
                rows = dst.shape[0]
                each = rows // parts
                dst[...] = full[:, at : at + each, :].reshape(rows, lanes)
                at += each
    (full_b, at_b), (full_c, at_c) = vecs
    col = outs[0].shape[2]
    me = place[1] * 2 + place[0]

    def small(first, second, attn, kernels, gains, shifts):
        for t in range(9):
            kernels[t, 0:1, :] = first[t : t + 1]
            kernels[t, 1:2, :] = second[t : t + 1]
        gains[0:1, :] = first[10:11]
        gains[1:2, :] = second[10:11]
        rows = [first[9:10], second[9:10], first[11:12], second[11:12]]
        rows += [first[r : r + 1] for r in attn] + [second[12:13], second[13:14]]
        for r, row in enumerate(rows):
            shifts[r : r + 1, :] = row

    c2, c1, s2, bias = [full_b[q, at_b : at_b + 16, :] for q in range(4)]
    rows = [full_c[q, at_c : at_c + 16, :] for q in range(full_c.shape[0])]
    while len(rows) > 1:
        rows = [a + b for a, b in zip(rows[0::2], rows[1::2])]
    s1 = pltpu.roll(rows[0], rows[0].shape[1] - me * col, 1)
    small(s1[:, 0:col], s2[:, 0:col], (12, 14), *outs[0:3])
    small(c1[:, 0:col], c2[:, 0:col], (12, 13, 14), *outs[4:7])
    share = outs[3].shape[1]
    outs[3][...] = bias[1:2, 0:share]
    outs[7][...] = bias[0:1, 0:share]


def group_unpack(place, groups, outs, name):
    pieces = [p for held, _ in groups for p in held]
    return pl.pallas_call(
        functools.partial(unpack_kernel, [(len(held), kinds) for held, kinds in groups]),
        grid_spec=pltpu.PrefetchScalarGridSpec(
            num_scalar_prefetch=1,
            grid=(1,),
            in_specs=[keep(p.shape) for p in pieces],
            out_specs=[keep(o) for o in outs],
            scratch_shapes=[
                pltpu.VMEM((len(held),) + held[0].shape, F32) for held, _ in groups
            ],
        ),
        out_shape=[jax.ShapeDtypeStruct(o, F32) for o in outs],
        compiler_params=pltpu.CompilerParams(
            dimension_semantics=("arbitrary",), vmem_limit_bytes=VMEM
        ),
        name=name,
    )(place, *pieces)


def together(*values):
    return lax.optimization_barrier(values)


def after(value, *others):
    return lax.optimization_barrier((value,) + others)[0]


def all_sum(small):
    for axis in ("core", "line", "img"):
        held = [small] + [exchange(small, axis, d) for d in range(1, lax.axis_size(axis))]
        while len(held) > 1:
            held = [a + b for a, b in zip(held[0::2], held[1::2])]
        small = held[0]
    return small


def image_sum(mine, other, beside=None):
    mine = mine + exchange(other, "core")
    held = [exchange(mine[d], "line", d) for d in range(1, mine.shape[0])]
    extra = None
    if beside is not None:
        extra = beside(mine)
        held = lax.optimization_barrier((held, extra))[0]
    return mine[0] + sum(held), extra


def image_gather(mine, lines_of, beside=None):
    held = [exchange(mine, "line", d) for d in range(1, lines_of)]
    extra = None
    if beside is not None:
        extra = beside(mine)
        held = lax.optimization_barrier((held, extra))[0]
    held = jnp.stack([mine] + held)
    return jnp.concatenate([held, exchange(held, "core")], axis=0), extra


def hold(shape):
    return pl.BlockSpec(
        shape, lambda i, *_: (0,) * len(shape), pipeline_mode=pl.Buffered(1)
    )


def keep(shape):
    return pl.BlockSpec(shape, lambda i, *_: (0,) * len(shape))


def lines(width):
    return pl.BlockSpec((LINES, COLS, width), lambda i, *_: (i, 0, 0))


def tokens(width, col=0):
    return pl.BlockSpec((CHUNK, width), lambda i, *_: (i, col))


def call(body, chunks, prefetch, args, in_specs, outs, out_specs, scratch, flops, name):
    size = sum(a.size * a.dtype.itemsize for a in args) + sum(
        functools.reduce(lambda a, b: a * b, o.shape) * o.dtype.itemsize for o in outs
    )
    return pl.pallas_call(
        body,
        grid_spec=pltpu.PrefetchScalarGridSpec(
            num_scalar_prefetch=len(prefetch),
            grid=(chunks,),
            in_specs=in_specs,
            out_specs=out_specs,
            scratch_shapes=scratch,
        ),
        out_shape=outs,
        compiler_params=pltpu.CompilerParams(
            dimension_semantics=("arbitrary",), vmem_limit_bytes=VMEM
        ),
        cost_estimate=pl.CostEstimate(flops=flops, bytes_accessed=size, transcendentals=0),
        name=name,
    )(*prefetch, *args)


def weight_grad(y, x, name):
    total, n = y.shape
    m = x.shape[1]
    step = 256
    return pl.pallas_call(
        weight_kernel,
        grid=(n // step,),
        in_specs=[pl.BlockSpec((total, step), lambda j: (0, j)), hold((total, m))],
        out_specs=pl.BlockSpec((step, m), lambda j: (j, 0)),
        out_shape=jax.ShapeDtypeStruct((n, m), BF16),
        compiler_params=pltpu.CompilerParams(
            dimension_semantics=("arbitrary",), vmem_limit_bytes=VMEM
        ),
        cost_estimate=pl.CostEstimate(
            flops=2 * total * n * m,
            bytes_accessed=2 * (total * (n + m) + n * m),
            transcendentals=0,
        ),
        name=name,
    )(y, x)


def shards(
    glob_x, loc_x, glob_cot, loc_cot, loc_extent, glob_image, loc_image,
    s_kernels, s_gains, s_shifts, s_qkv, s_proj, s_fc1, s_fc1_bias, s_fc2,
    c_kernels, c_gains, c_shifts, c_qkv, c_proj, c_fc1, c_fc1_bias, c_fc2,
):
    globs, locs = glob_x.shape[0], loc_x.shape[0]
    width = glob_x.shape[3]
    hidden = s_fc1.shape[1]
    chunks = globs + locs // WPC
    total = chunks * CHUNK
    parts, lines_of = lax.axis_size("img"), lax.axis_size("line")
    groups = 2 * lines_of
    images = glob_image.shape[0] // 2
    per = images // groups
    core, line = lax.axis_index("core"), lax.axis_index("line")
    me = 2 * line + core
    place = jnp.stack([core, line, lax.axis_index("img"), jnp.int32(lines_of)])
    scalars = (place, glob_image, loc_image, loc_extent.T)
    s_vecs = (s_kernels.transpose(1, 0, 2), s_gains, s_shifts)
    c_vecs = (c_kernels.transpose(1, 0, 2), c_gains, c_shifts)

    def f3(w=width):
        return jax.ShapeDtypeStruct((total // COLS, COLS, w), F32)

    def b2(w=width):
        return jax.ShapeDtypeStruct((total, w), BF16)

    def sh(*shape):
        return jax.ShapeDtypeStruct(shape, F32)

    glob_spec = pl.BlockSpec(
        (1, 14, 14, width), lambda i, *_: (jnp.minimum(i, globs - 1), 0, 0, 0)
    )
    loc_spec = pl.BlockSpec(
        (WPC, WIN, WIN, width), lambda i, *_: (jnp.maximum(i - globs, 0), 0, 0, 0)
    )
    s_wide = pltpu.VMEM((14, 16, width), F32)
    s_tok = pltpu.VMEM((LINES, COLS, width), F32)
    s_valid = pltpu.VMEM((LINES, COLS, LANES), F32)
    s_vec = pltpu.VMEM((32, width), F32)
    s_gram = pltpu.VMEM((images, HEAD_DIM, width), F32)
    s_acc = pltpu.VMEM((16, COLS, width), F32)
    s_bias = pltpu.VMEM((COLS, hidden), F32)

    def s_flat(w):
        return pltpu.VMEM((CHUNK, w), F32)

    s_specs, c_specs = [hold(v.shape) for v in s_vecs], [hold(v.shape) for v in c_vecs]
    half_sums = sh(lines_of, per * HEAD_DIM, width)
    gram_spec = hold((images, HEAD_DIM, width))
    w_qkv, w_proj = hold((width, 3 * width)), hold((width, width))
    w_fc1, w_fc2 = hold((width, hidden)), hold((hidden, width))
    dense = 2 * total * width * (4 * width + 2 * hidden)
    probs_shape = (chunks * WPC, width // LANES, COLS * COLS, 2 * LANES)
    probs_spec = pl.BlockSpec((WPC,) + probs_shape[1:], lambda i, *_: (i, 0, 0, 0))

    (c1, h1, p, o, c2, c3, h2, g, gp, mid, cc1, ch1, cp, probs_s, gram_a, gram_b) = call(
        functools.partial(spatial_kernel, globs), chunks, scalars,
        (glob_x, loc_x, *s_vecs, *c_vecs, s_fc1_bias.reshape(1, -1), s_qkv, s_proj, s_fc1, s_fc2,
         c_qkv),
        [glob_spec, loc_spec, *s_specs, *c_specs, hold((1, hidden)), w_qkv, w_proj, w_fc1, w_fc2,
         w_qkv],
        [f3(), b2(), b2(3 * width), b2(), f3(), f3(), b2(), b2(hidden), b2(hidden), f3(), f3(),
         b2(), b2(3 * width), sh(*probs_shape), half_sums, half_sums],
        [lines(width), tokens(width), tokens(3 * width), tokens(width), lines(width),
         lines(width), tokens(width), tokens(hidden), tokens(hidden), lines(width), lines(width),
         tokens(width), tokens(3 * width), probs_spec, keep(half_sums.shape),
         keep(half_sums.shape)],
        [s_wide, s_tok, s_valid, s_flat(3 * width), s_flat(width), s_gram, s_vec, s_vec],
        dense + 6 * total * width * width, "spatial_fwd",
    )

    def beside_cot(ready):
        return call(
            functools.partial(cot_kernel, globs), chunks, scalars[:1],
            (after(glob_cot, ready), loc_cot, c_fc2),
            [glob_spec, loc_spec, w_fc2],
            [b2(), b2(hidden), sh(16, width)],
            [tokens(width), tokens(hidden), keep((16, width))],
            [s_wide, s_tok, s_acc],
            2 * total * width * hidden, "channel_cot",
        )

    def beside_turn(ready):
        return turned_weights(s_fc1, s_fc2, after(c_fc1, ready))

    scores, (dout, cdg, cvec0) = image_sum(gram_a, gram_b, beside_cot)
    scores = scores.reshape(per, HEAD_DIM, width) * channel_scale()
    exponent = jnp.exp(scores - jnp.max(scores, axis=1, keepdims=True))
    probs = exponent / jnp.sum(exponent, axis=1, keepdims=True)
    packed = (per * HEAD_DIM, width)
    a_all, (s_fc1_t, s_fc2_t, c_fc1_t) = image_gather(
        probs.astype(BF16).reshape(packed), lines_of, beside_turn
    )
    a_all = a_all.reshape(images, HEAD_DIM, width)

    (glob_out, loc_out, co, ch2, cg, cdu, dc2, cdob, cdo, gram_a, gram_b, cvec2, cbias) = call(
        functools.partial(channel_kernel, globs), chunks, scalars,
        (a_all, cc1, cp, dout, cdg, cvec0, *c_vecs, c_fc1_bias.reshape(1, -1), c_proj, c_fc1,
         c_fc1_t, c_fc2),
        [gram_spec, lines(width), tokens(width, 2), tokens(width), tokens(hidden),
         hold((16, width)), *c_specs, hold((1, hidden)), w_proj, w_fc1, w_fc2, w_fc2],
        [jax.ShapeDtypeStruct(glob_x.shape, BF16), jax.ShapeDtypeStruct(loc_x.shape, BF16),
         b2(), b2(), b2(hidden), b2(hidden), f3(), b2(), b2(),
         half_sums, half_sums, sh(16, width), sh(1, hidden)],
        [glob_spec, loc_spec, tokens(width), tokens(width), tokens(hidden), tokens(hidden),
         lines(width), tokens(width), tokens(width),
         keep(half_sums.shape), keep(half_sums.shape), keep((16, width)), keep((1, hidden))],
        [s_wide, s_tok, s_valid, s_tok, s_tok, s_flat(hidden),
         s_flat(width), s_gram, s_acc, s_bias, s_vec],
        2 * dense, "channel_mid",
    )

    direct = parts == 4 and lines_of == 4 and 4 * width == hidden
    grads = functools.partial(group_grad, place, lanes=width, lines_of=lines_of, parts=parts)

    def scatter(array, axis):
        return lax.psum_scatter(array, axis, scatter_dimension=0, tiled=True)[0]

    def beside_a1(ready):
        pairs = [(after(cdu, ready), ch2)]
        return grads(pairs, ("side",), "one", blocks=(0, 2), name="c_fc1_grads")[0]

    def beside_a2(ready):
        pairs = [(after(dout, ready), cg)]
        return grads(
            pairs, ("rows",), "one", blocks=(1, 2), base=buffer_a1, name="c_fc2_grads"
        )[0]

    dprobs, buffer_a1 = image_sum(gram_a, gram_b, beside_a1 if direct else None)
    dprobs = dprobs.reshape(per, HEAD_DIM, width)
    dscores = probs * (dprobs - jnp.sum(dprobs * probs, axis=1, keepdims=True))
    ds_all, buffer_a = image_gather(
        dscores.astype(BF16).reshape(packed), lines_of, beside_a2 if direct else None
    )
    ds_all = ds_all.reshape(images, HEAD_DIM, width)
    if direct:
        ds_all, buffer_a = together(ds_all, buffer_a)
        piece_a = scatter(buffer_a, "core")

    (cdp, dmid, cvec1) = call(
        functools.partial(channel_back_kernel, globs), chunks, scalars,
        (a_all, ds_all, cp, cdo, dc2, cc1, mid, *c_vecs, c_qkv),
        [gram_spec, gram_spec, tokens(3 * width), tokens(width), lines(width), lines(width),
         lines(width), *c_specs, w_qkv],
        [b2(3 * width), f3(), sh(16, width)],
        [tokens(3 * width), lines(width), keep((16, width))],
        [s_tok, s_valid, s_flat(width), s_acc, s_vec],
        6 * total * width * width, "channel_back",
    )

    kinds_a, kinds_c = ("side", "rows"), ("cols",)
    kinds_s = ("cols", "cols", "side", "rows", "cols", "vec")
    if direct:
        dmid, piece_a = together(dmid, piece_a)
        piece_a = scatter(piece_a, "img")

    (du, dmb, dob, sdc2, sdo, svec2, sbias) = call(
        functools.partial(hidden_back_kernel, globs), chunks, scalars,
        (c2, c3, gp, dmid, *s_vecs, s_proj, s_fc1_t, s_fc2_t),
        [lines(width), lines(width), tokens(hidden), lines(width), *s_specs, w_proj, w_fc2,
         w_fc1],
        [b2(hidden), b2(), b2(), f3(), b2(), sh(16, width), sh(1, hidden)],
        [tokens(hidden), tokens(width), tokens(width), lines(width), tokens(width),
         keep((16, width)), keep((1, hidden))],
        [s_tok, s_valid, s_flat(width), s_acc, s_bias, s_vec],
        2 * total * width * (2 * hidden + width), "hidden_back",
    )
    if direct:
        mine, other = grads(
            [(cdp, ch1), (cdob, co), (du, h2), (dmb, g), (dob, o),
             (cvec2, cvec1, svec2, cbias, sbias)],
            kinds_s, "pair", name="s_fc_grads",
        )
        sdo, mine, other, piece_a = together(sdo, mine, other, piece_a)
        piece_a = scatter(piece_a, "line")
        got = exchange(other, "core")

    dp, svec3 = window_back(probs_s, p, sdo, 0, 2, None)
    if direct:
        dp, got = together(dp, got)
        keep_a, send_a, keep_b, send_b = halved_core(mine, got)
        got_a, got_b = exchange(send_a, "img", 1), exchange(send_b, "img", 2)
        dp = after(dp, keep_a)
    dp, svec3 = window_back(probs_s, p, sdo, 2, chunks - 2, (dp, svec3))
    if direct:
        mine, other = grads([(dp, h1)], kinds_c, "xor", hint=0, name="s_qkv_grads")
        mine, other, got_a, got_b, piece_a = together(mine, other, got_a, got_b, piece_a)
        quarters_a = quarters(piece_a)
        pieces_c = group_sum_core(mine, other, "c")
        keep_a, send_a, keep_b, send_b = halved_first(keep_a, got_a, keep_b, got_b)
        got_a, got_b = exchange(send_a, "img", 2), exchange(send_b, "img", 1)
        held_c = [pieces_c[0]] + [exchange(pieces_c[d], "img", d) for d in range(1, parts)]
        keep_a, got_a, got_b, first_c = together(keep_a, got_a, got_b, pieces_c[0])
        piece_s = halved_second(keep_a, got_a, keep_b, got_b)
        dp, piece_s = together(dp, piece_s)
        piece_s = scatter(piece_s, "line")

    (glob_grad, loc_grad, svec1) = call(
        functools.partial(first_back_kernel, globs), chunks, scalars,
        (glob_x, loc_x, c1, dp, sdc2, *s_vecs, s_qkv, svec3),
        [glob_spec, loc_spec, lines(width), tokens(3 * width), lines(width), *s_specs, w_qkv,
         hold((16, width))],
        [jax.ShapeDtypeStruct(glob_x.shape, F32), jax.ShapeDtypeStruct(loc_x.shape, F32),
         sh(16, width)],
        [glob_spec, loc_spec, keep((16, width))],
        [s_wide, s_tok, s_tok, s_valid, s_flat(width), s_acc, s_vec],
        6 * total * width * width, "first_back",
    )

    share, col = hidden // groups, width // groups
    if direct:
        cut = (lines_of, -1, width)
        svec1, *quarters_a = together(svec1, *quarters_a)
        vectors = [svec1, exchange(svec1, "core")]
        pieces = sum_with_vectors([v.reshape(cut) for v in held_c], vectors, "c_sum_img")
        piece_c = group_sum_line(pieces, "c")
        quarters_s = quarters(after(piece_s, pieces[0]))
        quarters_c = quarters(piece_c)
        small = [(9, 2, col), (2, col)]
        (c_fc1_g, c_fc2_g, c_qkv_g, c_proj_g, s_fc1_g, s_fc2_g, s_proj_g, s_qkv_g,
         s_ker, s_gain, s_shift, s_bias, c_ker, c_gain, c_shift, c_bias) = group_unpack(
            place,
            [(quarters_a, kinds_a), (quarters_s, kinds_s), (quarters_c, kinds_c + ("late",))],
            [(width, share), (col, hidden), (3 * col, width), (col, width), (width, share),
             (col, hidden), (col, width), (3 * col, width)]
            + small + [(8, col), (1, share)] + small + [(9, col), (1, share)],
            "grads_out",
        )
        s_ker, c_ker = s_ker.transpose(1, 0, 2), c_ker.transpose(1, 0, 2)
        s_bias, c_bias = s_bias.reshape(share), c_bias.reshape(share)
    else:

        def reduced(y, x):
            grad = weight_grad(y, x, "weight_grad")
            mine = lax.psum_scatter(grad, GRP, scatter_dimension=0, tiled=True)
            return lax.psum(mine, "img").astype(F32)

        c_fc1_g, c_proj_g, c_fc2_g = reduced(cdu, ch2).T, reduced(cdob, co), reduced(dout, cg)
        c_qkv_g, s_fc1_g, s_fc2_g = reduced(cdp, ch1), reduced(du, h2).T, reduced(dmb, g)
        s_qkv_g, s_proj_g = reduced(dp, h1), reduced(dob, o)
        rows = [all_sum(v) for v in (cvec2, cvec1, svec2, svec1)]
        c2v, c1v, s2v, s1v = [lax.dynamic_slice(v, (0, me * col), (16, col)) for v in rows]
        c_bias, s_bias = [
            lax.dynamic_slice(all_sum(v)[0], (me * share,), (share,)) for v in (cbias, sbias)
        ]

        def small_grads(first, second, attn):
            kernels = jnp.stack([first[0:9], second[0:9]])
            shifts = [first[9], second[9], first[11], second[11], *attn, second[12], second[13]]
            return kernels, jnp.stack([first[10], second[10]]), jnp.stack(shifts)

        c_ker, c_gain, c_shift = small_grads(c1v, c2v, [c1v[12], c1v[13], c1v[14]])
        s_ker, s_gain, s_shift = small_grads(s1v, s2v, [s1v[12], s1v[14]])
    return (
        glob_out, loc_out, glob_grad, loc_grad,
        s_ker, s_gain, s_shift, s_qkv_g.T, s_proj_g.T, s_fc1_g, s_bias, s_fc2_g.T,
        c_ker, c_gain, c_shift, c_qkv_g.T, c_proj_g.T, c_fc1_g, c_bias, c_fc2_g.T,
    )


def solution(mesh):
    whole = jax.sharding.Mesh(
        mesh.devices.reshape(mesh.shape["img"], mesh.shape["grp"] // 2, 2), ("img", *GRP)
    )
    every = ("img", *GRP)
    maps = P(every, None, None, None)
    weight_outs = (
        P(None, None, GRP), P(None, GRP), P(None, GRP), P(None, GRP), P(None, GRP),
        P(None, GRP), P(GRP), P(None, GRP),
    )
    return jax.shard_map(
        shards,
        mesh=whole,
        in_specs=(maps,) * 4 + (P(every, None), P("img"), P("img")) + (P(),) * 16,
        out_specs=(maps,) * 4 + weight_outs * 2,
        check_vma=False,
    )
```

time: 1350 us -> 369 us (0.27)
  local copies, waits for them, and re-layouts: 399 us -> 16.1 us
  waiting for transfers between devices: 368 us -> 31.8 us
  Pallas kernels: 0 us -> 259 us
  matrix products: 251 us -> 0 us
  other arithmetic: 201 us -> 3.39 us
  blocking collectives: 69.1 us -> 0 us
    pallas_call x0 -> x20, Pallas kernels: none -> 259 us  [the longest x6 162 us: call(): pl.pallas_call(body, grid_spec=pltpu.PrefetchScalarGridSpec(num_scalar_pr...]
    dot_general x40 -> x0, matrix products: 251 us -> none  [the longest x8 48.1 us: input_grad(): lax.dot_general(upstream, weight, (((1,), (1,)), ((), ())), preferred_ele...]
    reshape x68 -> x2, local copies, waits for them, and re-layouts: 198 us -> 1.9 us  [the longest x1 1.29 us: shards(): s_fc1_bias.reshape(1, -1)]
    all_to_all x7 -> x0, waiting for transfers between devices: 165 us -> none  [the longest x1 35.4 us: channel_back(): lax.all_to_all(grads_back[1].reshape(-1, piece_width), 'grp', split_axis=...]
    unnamed x21 -> x5, waiting for transfers between devices: 143 us -> 0.08 us
    reduce_sum x41 -> x1, other arithmetic: 109 us -> 0.05 us  [shards(): probs = exponent / jnp.sum(exponent, axis=1, keepdims=True)]
    ppermute x0 -> x38, starting transfers between devices: none -> 42.9 us  [exchange(): return lax.ppermute(array, axis, [(i, i ^ flip) for i in range(size)])]
    psum x1 -> x0, waiting for transfers between devices: 42.2 us -> none  [shards(): lax.psum(shares[3].astype(jnp.bfloat16), 'img').astype(jnp.float32)]
  transfers between devices with their start and end apart: 22 -> 42, of which waited for: 13 -> 15; matrix products, arithmetic and copies ran while one was open for 32% -> 1% of each run, Pallas kernels for 0% -> 44%
where the time goes in v1:
time: 369 us; the launch traced here: 367 us
  Pallas kernels  259 us (70%)
  starting transfers between devices  43 us (12%)
  waiting for transfers between devices  31.8 us (9%)
  local copies, waits for them, and re-layouts  16.1 us (4%)
  between operations  14.3 us (4%)
    pallas_call x6, Pallas kernels, call(): pl.pallas_call(body, grid_spec=pltpu.PrefetchScalarGridSpec(num_scalar_pr...  162 us
    pallas_call x4, Pallas kernels, group_grad(): pl.pallas_call(functools.partial(group_kernel, kinds, counts, mode, 0 if...  51.8 us
    ppermute x38, starting transfers between devices, exchange(): return lax.ppermute(array, axis, [(i, i ^ flip) for i in range(size)])  42.9 us
    ppermute x38, waiting for transfers between devices, exchange(): return lax.ppermute(array, axis, [(i, i ^ flip) for i in range(size)])  31.7 us
    pallas_call x2, Pallas kernels, window_back(): pl.pallas_call(window_back_kernel, grid=(count,), in_specs=specs, out_spe...  15.8 us
    pallas_call x4, Pallas kernels, small_call(): pl.pallas_call(body, grid=grid, in_specs=in_specs, out_specs=out_specs, o...  15.2 us
    unnamed x69, local copies, waits for them, and re-layouts  13 us
  transfers between devices with their start and end apart: 42, of which 15 were waited for; matrix products, arithmetic and copies ran while one was open for 1% of the time, Pallas kernels for 44%

profile of v1, /device:TPU:0, one launch (start us, length us, event | category | flops | bytes accessed | tf_op | source)
XLA Modules:
  0.0 367.5 jit_solution(12194077167475274979)
XLA Ops:
  8.5 2.3 copy.50.gx
  11.4 48.2 %spatial_fwd.1 = (f32[196,8,512]{2,1,0:T(8,128)}, bf16[1568,512]{1,0:T(8,128)(2,1)}, bf16[1568,1536]{1,0:T(8,128)(2,1)}, bf16[1568,512]{1,0:T(8,128)(2,1)}, f32[...) custom-call(s32[4]{0:T(128)} %pad_add_fusion.place, ...), custom_call_target="tpu_custom_call" | custom-call | flops 12331253760 | bytes 62678016 | tf_op jit(solution)/shard_map/spatial_fwd/pallas_call | solution.py:1220
  60.1 1.7 collective-permute-done
  63.0 5.0 %collective-permute-start.3 = (f32[64,512]{1,0:T(8,128)S(1)}, f32[64,512]{1,0:T(8,128)S(1)}, u32[]{:S(2)}, u32[]{:S(2)}) collective-permute-start(f32[64,512]{1,0:T(8,128)S(1)} %get-tuple-element.327), channel_id=1, source_target_pairs={{0,6},{2,4},{4,2},{6,0},{1,7},{3,5},{5,3},{7,1},{8,14},{10,12},{12... | collective-permute-start | bytes 393224 | tf_op jit(solution)/shard_map/ppermute | solution.py:1060
  69.8 11.0 %channel_cot.1 = (bf16[1568,512]{1,0:T(8,128)(2,1)}, bf16[1568,2048]{1,0:T(8,128)(2,1)}, f32[16,512]{1,0:T(8,128)}) custom-call(s32[4]{0:T(128)} %pad_add_fusion.place, bf16[4,14,14,512]{3,2,1,0:T(8,128)(2,1)} %copy.51.gcot, bf16[12,7,7,512]{3,2,1,0:T(8,128)(2,1)} %lcot.1, bf16[2048,512]{1,0:T(8,128)(2,1)} %w2.5), custom_call_target="tpu_custom_call" | custom-call | flops 3288334336 | bytes 11563008 | tf_op jit(solution)/shard_map/channel_cot/pallas_call | solution.py:1220
  81.0 3.8 %collective-permute-start.6 = (bf16[64,512]{1,0:T(8,128)(2,1)S(1)}, bf16[64,512]{1,0:T(8,128)(2,1)S(1)}, u32[]{:S(2)}, u32[]{:S(2)}) collective-permute-start(bf16[64,512]{1,0:T(8,128)(2,1)S(1)} %get-tuple-element.331), channel_id=1, source_target_pairs={{0,6},{2,4},{4,2},{6,0},{1,7},{3,5},{5,3},{7,1},{8,14},{10,12},{12... | collective-permute-start | bytes 196616 | tf_op jit(solution)/shard_map/ppermute | solution.py:1060
  86.1 6.1 %turned_weights.1 = (bf16[2048,512]{1,0:T(8,128)(2,1)}, bf16[512,2048]{1,0:T(8,128)(2,1)}, bf16[2048,512]{1,0:T(8,128)(2,1)}) custom-call(bf16[512,2048]{1,0:T(8,128)(2,1)} %refs_0_.1, bf16[2048,512]{1,0:T(8,128)(2,1)} %refs_1_.1, bf16[512,2048]{1,0:T(8,128)(2,1)} %w1.3), custom_call_target="tpu_custom_call" | custom-call | tf_op jit(solution)/shard_map/turned_weights/pallas_call | solution.py:628
  92.4 1.5 collective-permute-done.7
  94.7 42.6 %channel_mid.1 = (bf16[4,14,14,512]{3,2,1,0:T(8,128)(2,1)}, bf16[12,7,7,512]{3,2,1,0:T(8,128)(2,1)}, bf16[1568,512]{1,0:T(8,128)(2,1)}, bf16[1568,512]{1,0:T(8,1...) custom-call(s32[4]{0:T(128)} %pad_add_fusion.place, ...), custom_call_target="tpu_custom_call" | custom-call | flops 19730006016 | bytes 48436224 | tf_op jit(solution)/shard_map/channel_mid/pallas_call | solution.py:1220
  137.6 2.0 collective-permute-done.8
  140.7 3.8 %collective-permute-start.11 = (f32[64,512]{1,0:T(8,128)S(1)}, f32[64,512]{1,0:T(8,128)S(1)}, u32[]{:S(2)}, u32[]{:S(2)}) collective-permute-start(f32[64,512]{1,0:T(8,128)S(1)} %get-tuple-element.324), channel_id=1, source_target_pairs={{0,6},{2,4},{4,2},{6,0},{1,7},{3,5},{5,3},{7,1},{8,14},{10,12},{12... | collective-permute-start | bytes 393224 | tf_op jit(solution)/shard_map/ppermute | solution.py:1060
  145.2 9.3 %c_fc1_grads.1.refs_2_ = bf16[2,4,4,128,512]{4,3,2,1,0:T(8,128)(2,1)} custom-call(s32[4]{0:T(128)} %pad_add_fusion.place, bf16[1568,2048]{1,0:T(8,128)(2,1)} %get-tuple-element.180.refs_0_, bf16[1568,512]{1,0:T(8,128)(2,1)} %get-tuple-element.181.refs_1_), custom_call_target="tpu_custom_call" | custom-call | flops 3288334336 | bytes 10125312 | tf_op jit(solution)/shard_map/c_fc1_grads/pallas_call | solution.py:923
  155.9 2.7 collective-permute-start.14
  158.6 1.7 collective-permute-start.12
  160.4 9.3 %c_fc2_grads.1 = bf16[2,4,4,128,512]{4,3,2,1,0:T(8,128)(2,1)} custom-call(s32[4]{0:T(128)} %pad_add_fusion.place, bf16[1568,512]{1,0:T(8,128)(2,1)} %get-tuple-element.185.dout.refs_0_, bf16[1568,2048]{1,0:T(8,128)(2,1)} %get-tuple-element.186.refs_1_, bf16[2,4,4,128,512]{4,3,2,1,0:T(8,128)(2,1)} %c_fc1_grads.1.refs_2_), custom_call_target="tpu_custom_call", output_to_operand_aliasing={{}: (3, {})} | custom-call | flops 3288334336 | bytes 14319616 | tf_op jit(solution)/shard_map/c_fc2_grads/pallas_call | solution.py:923
  169.9 1.5 collective-permute-done.15
  172.2 20.7 %channel_back.1 = (bf16[1568,1536]{1,0:T(8,128)(2,1)}, f32[196,8,512]{2,1,0:T(8,128)}, f32[16,512]{1,0:T(8,128)}) custom-call(s32[4]{0:T(128)} %pad_add_fusion.place, s32[32]{0:T(128)} %gi.9, s32[96]{0:T(128)} %li.9, s32[2,12]{1,0:T(2,128)} %bitcast.150, bf16[16,32,512]{2,1,0:T(8,128)(2,1)} %bitcast.114, bf16[16,32,512]{2,1,0:T(8,128)(2,1)} %bitcast.115, ...), custom_call_target="tpu_custom_call" | custom-call | flops 2466250752 | bytes 26768384 | tf_op jit(solution)/shard_map/channel_back/pallas_call | solution.py:1220
  193.0 22.0 %hidden_back.1 = (bf16[1568,2048]{1,0:T(8,128)(2,1)}, bf16[1568,512]{1,0:T(8,128)(2,1)}, bf16[1568,512]{1,0:T(8,128)(2,1)}, f32[196,8,512]{2,1,0:T(8,128)}, bf16...) custom-call(s32[4]{0:T(128)} %pad_add_fusion.place, s32[32]{0:T(128)} %gi.9, s32[96]{0:T(128)} %li.9, ...), custom_call_target="tpu_custom_call" | custom-call | flops 7398752256 | bytes 35295232 | tf_op jit(solution)/shard_map/hidden_back/pallas_call | solution.py:1220
  215.0 25.3 %s_fc_grads.1 = (bf16[4,4,224,512]{3,2,1,0:T(8,128)(2,1)}, bf16[4,4,224,512]{3,2,1,0:T(8,128)(2,1)}) custom-call(s32[4]{0:T(128)} %pad_add_fusion.place, bf16[1568,1536]{1,0:T(8,128)(2,1)} %get-tuple-element.198.refs_0_, bf16[1568,512]{1,0:T(8,128)(2,1)} %get-tuple-element.199.refs_1_, bf16[1568,512]{1,0:T(8,128)(2,1)} %get-tuple-element.200.refs_2_, ...), custom_call_target="tpu_custom_call" | custom-call | flops 10687086592 | bytes 36356096 | tf_op jit(solution)/shard_map/s_fc_grads/pallas_call | solution.py:923
  240.7 5.4 %window_back.2 = (bf16[1568,1536]{1,0:T(8,128)(2,1)}, f32[16,512]{1,0:T(8,128)}) custom-call(f32[28,4,64,256]{3,2,1,0:T(8,128)} %get-tuple-element.172.probs, bf16[1568,1536]{1,0:T(8,128)(2,1)} %get-tuple-element.173.p, bf16[1568,512]{1,0:T(8,128)(2,1)} %get-tuple-element.216.do), custom_call_target="tpu_custom_call" | custom-call | flops 939524096 | bytes 5767168 | tf_op jit(solution)/shard_map/window_back/pallas_call | solution.py:706
  247.2 5.6 %s_sum_core.1 = (bf16[2,4,112,512]{3,2,1,0:T(8,128)(2,1)}, bf16[2,4,112,512]{3,2,1,0:T(8,128)(2,1)}, bf16[2,4,112,512]{3,2,1,0:T(8,128)(2,1)}, bf16[2,4,112,512]{3,2,1,0:T(8,128)(2,1)}) custom-call(bf16[4,4,224,512]{3,2,1,0:T(8,128)(2,1)} %get-tuple-element.221.a, bf16[4,4,224,512]{3,2,1,0:T(8,128)(2,1)} %collective-permute-done.16.b), custom_call_target="tpu_custom_call" | custom-call | tf_op jit(solution)/shard_map/s_sum_core/pallas_call | solution.py:972
  252.8 1.6 collective-permute-start.17
  254.4 1.5 collective-permute-start.18
  255.9 10.5 %window_back.3 = (bf16[1568,1536]{1,0:T(8,128)(2,1)}, f32[16,512]{1,0:T(8,128)}) custom-call(f32[28,4,64,256]{3,2,1,0:T(8,128)} %get-tuple-element.172.probs, bf16[1568,1536]{1,0:T(8,128)(2,1)} %get-tuple-element.173.p, bf16[1568,512]{1,0:T(8,128)(2,1)} %get-tuple-element.216.do, ...), custom_call_target="tpu_custom_call", output_to_operand_aliasing={{0}: (4, {})} | custom-call | flops 2348810240 | bytes 14417920 | tf_op jit(solution)/shard_map/window_back/pallas_call | solution.py:706
  266.4 7.8 %s_qkv_grads.1 = (bf16[4,4,48,512]{3,2,1,0:T(8,128)(2,1)}, bf16[4,4,48,512]{3,2,1,0:T(8,128)(2,1)}) custom-call(s32[4]{0:T(128)} %pad_add_fusion.place, bf16[1568,1536]{1,0:T(8,128)(2,1)} %get-tuple-element.245.refs_0_.dp, bf16[1568,512]{1,0:T(8,128)(2,1)} %get-tuple-element.226.refs_1_), custom_call_target="tpu_custom_call" | custom-call | tf_op jit(solution)/shard_map/s_qkv_grads/pallas_call | solution.py:923
  275.4 1.3 collective-permute-done.18.rb
  277.7 4.1 %s_sum_first.1 = (bf16[4,112,512]{2,1,0:T(8,128)(2,1)}, bf16[4,112,512]{2,1,0:T(8,128)(2,1)}, bf16[4,112,512]{2,1,0:T(8,128)(2,1)}, bf16[4,112,512]{2,1,0:T(8,128)(2,1)}) custom-call(bf16[2,4,112,512]{3,2,1,0:T(8,128)(2,1)} %get-tuple-element.223.a, bf16[2,4,112,512]{3,2,1,0:T(8,128)(2,1)} %copy-done.1, bf16[2,4,112,512]{3,2,1,0:T(8,128)(2,1)} %get-tuple-element.233.b, ...), custom_call_target="tpu_custom_call" | custom-call | tf_op jit(solution)/shard_map/s_sum_first/pallas_call | solution.py:972
  281.8 1.6 collective-permute-start.19
  284.8 2.3 c_sum_core.1
  287.2 6.9 %collective-permute-done.19.ra = bf16[4,112,512]{2,1,0:T(8,128)(2,1)S(1)} collective-permute-done((bf16[4,112,512]{2,1,0:T(8,128)(2,1)}, bf16[4,112,512]{2,1,0:T(8,128)(2,1)S(1)}, u32[]{:S(2)}, u32[]{:S(2)}) %collective-permute-start.19) | collective-permute-done | bytes 458784 | tf_op jit(solution)/shard_map/ppermute | solution.py:1060
  296.1 3.6 s_sum_second.1
  300.2 1.6 collective-permute-start.23
  301.8 1.5 collective-permute-start.22
  304.3 2.9 collective-permute-done.24.refs_3_
  307.5 17.4 %first_back.1 = (f32[4,14,14,512]{3,2,1,0:T(8,128)}, f32[12,7,7,512]{3,2,1,0:T(8,128)}, f32[16,512]{1,0:T(8,128)}) custom-call(s32[4]{0:T(128)} %pad_add_fusion.place, s32[32]{0:T(128)} %gi.9, s32[96]{0:T(128)} %li.9, s32[2,12]{1,0:T(2,128)} %bitcast.152, bf16[4,14,14,512]{3,2,1,0:T(8,128)(2,1)} %copy.50.gx, bf16[12,7,7,512]{3,2,1,0:T(8,128)(2,1)} %lx.3, ...), custom_call_target="tpu_custom_call" | custom-call | flops 2466250752 | bytes 17121280 | tf_op jit(solution)/shard_map/first_back/pallas_call | solution.py:1220
  325.1 1.4 collective-permute-done.28.refs_5_
  327.3 2.0 c_sum_img.1
  329.4 2.6 collective-permute-start.31
  332.9 3.3 collective-permute-start.33
  337.1 3.4 collective-permute-done.33
  340.5 2.0 collective-permute-done.34
  343.1 1.6 c_sum_line.1.refs_8_
  344.7 2.5 collective-permute-start.37
  347.7 2.4 collective-permute-done.37.refs_11_
  350.1 1.6 collective-permute-start.35
  351.7 1.5 copy.53
  353.2 2.2 copy.54
  356.9 4.0 %grads_out.1 = (f32[512,256]{1,0:T(8,128)}, f32[64,2048]{1,0:T(8,128)}, f32[192,512]{1,0:T(8,128)}, f32[64,512]{1,0:T(8,128)}, f32[512,256]{1,0:T(8,128)}, /*ind...) custom-call(s32[4]{0:T(128)} %pad_add_fusion.place, ...), custom_call_target="tpu_custom_call" | custom-call | tf_op jit(solution)/shard_map/grads_out/pallas_call | solution.py:1142
  (147 shorter events, 26.5 us)
Async XLA Ops:
  7.2 185.7 %reduce-scatter.7.cloned.1.call-start = ((), (), s32[]{:S(2)}) async-start(), calls=%async_computation.4 | async-start | bytes 6291456 | tf_op jit(solution)/shard_map/reduce_scatter | solution.py:1377
  11.4 57.3 %copy-start.4 = (bf16[4,14,14,512]{3,0,2,1:T(4,128)(2,1)S(1)}, bf16[4,14,14,512]{3,0,2,1:T(4,128)(2,1)}, u32[]{:S(2)}) copy-start(bf16[4,14,14,512]{3,0,2,1:T(4,128)(2,1)} %param.25) | copy-start | bytes 2408452
  59.6 2.3 collective-permute-start
  63.0 17.8 %collective-permute-start.3 = (f32[64,512]{1,0:T(8,128)S(1)}, f32[64,512]{1,0:T(8,128)S(1)}, u32[]{:S(2)}, u32[]{:S(2)}) collective-permute-start(f32[64,512]{1,0:T(8,128)S(1)} %get-tuple-element.327), channel_id=1, source_target_pairs={{0,6},{2,4},{4,2},{6,0},{1,7},{3,5},{5,3},{7,1},{8,14},{10,12},{12... | collective-permute-start | bytes 393224 | tf_op jit(solution)/shard_map/ppermute | solution.py:1060
  68.1 12.8 %collective-permute-start.2 = (f32[64,512]{1,0:T(8,128)S(1)}, f32[64,512]{1,0:T(8,128)S(1)}, u32[]{:S(2)}, u32[]{:S(2)}) collective-permute-start(f32[64,512]{1,0:T(8,128)S(1)} %get-tuple-element.328), channel_id=1, source_target_pairs={{0,4},{2,6},{4,0},{6,2},{1,5},{3,7},{5,1},{7,3},{8,12},{10,14},{12... | collective-permute-start | bytes 393224 | tf_op jit(solution)/shard_map/ppermute | solution.py:1060
  68.1 12.8 %collective-permute-start.1 = (f32[64,512]{1,0:T(8,128)S(1)}, f32[64,512]{1,0:T(8,128)S(1)}, u32[]{:S(2)}, u32[]{:S(2)}) collective-permute-start(f32[64,512]{1,0:T(8,128)S(1)} %get-tuple-element.329), channel_id=1, source_target_pairs={{0,2},{2,0},{4,6},{6,4},{1,3},{3,1},{5,7},{7,5},{8,10},{10,8},{12,... | collective-permute-start | bytes 393224 | tf_op jit(solution)/shard_map/ppermute | solution.py:1060
  81.0 11.2 %collective-permute-start.6 = (bf16[64,512]{1,0:T(8,128)(2,1)S(1)}, bf16[64,512]{1,0:T(8,128)(2,1)S(1)}, u32[]{:S(2)}, u32[]{:S(2)}) collective-permute-start(bf16[64,512]{1,0:T(8,128)(2,1)S(1)} %get-tuple-element.331), channel_id=1, source_target_pairs={{0,6},{2,4},{4,2},{6,0},{1,7},{3,5},{5,3},{7,1},{8,14},{10,12},{12... | collective-permute-start | bytes 196616 | tf_op jit(solution)/shard_map/ppermute | solution.py:1060
  84.8 7.4 %collective-permute-start.5 = (bf16[64,512]{1,0:T(8,128)(2,1)S(1)}, bf16[64,512]{1,0:T(8,128)(2,1)S(1)}, u32[]{:S(2)}, u32[]{:S(2)}) collective-permute-start(bf16[64,512]{1,0:T(8,128)(2,1)S(1)} %get-tuple-element.331), channel_id=1, source_target_pairs={{0,4},{2,6},{4,0},{6,2},{1,5},{3,7},{5,1},{7,3},{8,12},{10,14},{12... | collective-permute-start | bytes 196616 | tf_op jit(solution)/shard_map/ppermute | solution.py:1060
  84.8 7.4 %collective-permute-start.4 = (bf16[64,512]{1,0:T(8,128)(2,1)S(1)}, bf16[64,512]{1,0:T(8,128)(2,1)S(1)}, u32[]{:S(2)}, u32[]{:S(2)}) collective-permute-start(bf16[64,512]{1,0:T(8,128)(2,1)S(1)} %get-tuple-element.331), channel_id=1, source_target_pairs={{0,2},{2,0},{4,6},{6,4},{1,3},{3,1},{5,7},{7,5},{8,10},{10,8},{12,... | collective-permute-start | bytes 196616 | tf_op jit(solution)/shard_map/ppermute | solution.py:1060
  92.3 1.6 collective-permute-start.7
  137.3 2.2 collective-permute-start.8
  140.7 13.7 %collective-permute-start.11 = (f32[64,512]{1,0:T(8,128)S(1)}, f32[64,512]{1,0:T(8,128)S(1)}, u32[]{:S(2)}, u32[]{:S(2)}) collective-permute-start(f32[64,512]{1,0:T(8,128)S(1)} %get-tuple-element.324), channel_id=1, source_target_pairs={{0,6},{2,4},{4,2},{6,0},{1,7},{3,5},{5,3},{7,1},{8,14},{10,12},{12... | collective-permute-start | bytes 393224 | tf_op jit(solution)/shard_map/ppermute | solution.py:1060
  144.5 11.0 %collective-permute-start.10 = (f32[64,512]{1,0:T(8,128)S(1)}, f32[64,512]{1,0:T(8,128)S(1)}, u32[]{:S(2)}, u32[]{:S(2)}) collective-permute-start(f32[64,512]{1,0:T(8,128)S(1)} %get-tuple-element.325), channel_id=1, source_target_pairs={{0,4},{2,6},{4,0},{6,2},{1,5},{3,7},{5,1},{7,3},{8,12},{10,14},{12... | collective-permute-start | bytes 393224 | tf_op jit(solution)/shard_map/ppermute | solution.py:1060
  144.5 11.0 %collective-permute-start.9 = (f32[64,512]{1,0:T(8,128)S(1)}, f32[64,512]{1,0:T(8,128)S(1)}, u32[]{:S(2)}, u32[]{:S(2)}) collective-permute-start(f32[64,512]{1,0:T(8,128)S(1)} %get-tuple-element.326), channel_id=1, source_target_pairs={{0,2},{2,0},{4,6},{6,4},{1,3},{3,1},{5,7},{7,5},{8,10},{10,8},{12,... | collective-permute-start | bytes 393224 | tf_op jit(solution)/shard_map/ppermute | solution.py:1060
  155.9 13.8 %collective-permute-start.14 = (bf16[64,512]{1,0:T(8,128)(2,1)S(1)}, bf16[64,512]{1,0:T(8,128)(2,1)S(1)}, u32[]{:S(2)}, u32[]{:S(2)}) collective-permute-start(bf16[64,512]{1,0:T(8,128)(2,1)S(1)} %get-tuple-element.333), channel_id=1, source_target_pairs={{0,6},{2,4},{4,2},{6,0},{1,7},{3,5},{5,3},{7,1},{8,14},{10,12},{12... | collective-permute-start | bytes 196616 | tf_op jit(solution)/shard_map/ppermute | solution.py:1060
  158.6 11.1 %collective-permute-start.13 = (bf16[64,512]{1,0:T(8,128)(2,1)S(1)}, bf16[64,512]{1,0:T(8,128)(2,1)S(1)}, u32[]{:S(2)}, u32[]{:S(2)}) collective-permute-start(bf16[64,512]{1,0:T(8,128)(2,1)S(1)} %get-tuple-element.333), channel_id=1, source_target_pairs={{0,4},{2,6},{4,0},{6,2},{1,5},{3,7},{5,1},{7,3},{8,12},{10,14},{12... | collective-permute-start | bytes 196616 | tf_op jit(solution)/shard_map/ppermute | solution.py:1060
  158.6 11.1 %collective-permute-start.12 = (bf16[64,512]{1,0:T(8,128)(2,1)S(1)}, bf16[64,512]{1,0:T(8,128)(2,1)S(1)}, u32[]{:S(2)}, u32[]{:S(2)}) collective-permute-start(bf16[64,512]{1,0:T(8,128)(2,1)S(1)} %get-tuple-element.333), channel_id=1, source_target_pairs={{0,2},{2,0},{4,6},{6,4},{1,3},{3,1},{5,7},{7,5},{8,10},{10,8},{12,... | collective-permute-start | bytes 196616 | tf_op jit(solution)/shard_map/ppermute | solution.py:1060
  169.8 1.6 collective-permute-start.15
  171.4 69.0 %reduce-scatter.13.cloned.1.call-start = ((), (), s32[]{:S(2)}) async-start(), calls=%async_computation.7 | async-start | bytes 2621440
  193.0 81.3 %reduce-scatter.9.cloned.1.call-start = ((), (), s32[]{:S(2)}) async-start(), calls=%async_computation.5 | async-start | bytes 655360 | tf_op jit(solution)/shard_map/reduce_scatter | solution.py:1377
  240.4 6.8 %collective-permute-start.16 = (bf16[4,4,224,512]{3,2,1,0:T(8,128)(2,1)}, bf16[4,4,224,512]{3,2,1,0:T(8,128)(2,1)}, u32[]{:S(2)}, u32[]{:S(2)}) collective-permute-start(bf16[4,4,224,512]{3,2,1,0:T(8,128)(2,1)} %get-tuple-element.219), channel_id=1, source_target_pairs={{0,1},{1,0},{2,3},{3,2},{4,5},{5,4},{6,7},{7,6},{8,9},{9,8},{10,11... | collective-permute-start | bytes 11010056 | tf_op jit(solution)/shard_map/ppermute | solution.py:1060
  240.7 88.8 %reduce-scatter.11.cloned.1.call-start = ((), (), s32[]{:S(2)}) async-start(), calls=%async_computation.6 | async-start | bytes 1146880 | tf_op jit(solution)/shard_map/reduce_scatter | solution.py:1377
  252.8 22.6 %collective-permute-start.17 = (bf16[2,4,112,512]{3,2,1,0:T(8,128)(2,1)}, bf16[2,4,112,512]{3,2,1,0:T(8,128)(2,1)S(1)}, u32[]{:S(2)}, u32[]{:S(2)}) collective-permute-start(bf16[2,4,112,512]{3,2,1,0:T(8,128)(2,1)} %get-tuple-element.229), channel_id=1, source_target_pairs={{0,8},{8,0},{16,24},{24,16},{1,9},{9,1},{17,25},{25,17},{2,10},{10... | collective-permute-start | bytes 2752520 | tf_op jit(solution)/shard_map/ppermute | solution.py:1060
  254.4 22.4 %collective-permute-start.18 = (bf16[2,4,112,512]{3,2,1,0:T(8,128)(2,1)}, bf16[2,4,112,512]{3,2,1,0:T(8,128)(2,1)S(1)}, u32[]{:S(2)}, u32[]{:S(2)}) collective-permute-start(bf16[2,4,112,512]{3,2,1,0:T(8,128)(2,1)} %get-tuple-element.230), channel_id=1, source_target_pairs={{0,16},{8,24},{16,0},{24,8},{1,17},{9,25},{17,1},{25,9},{2,18},{10... | collective-permute-start | bytes 2752520 | tf_op jit(solution)/shard_map/ppermute | solution.py:1060
  276.8 7.2 %collective-permute-start.21 = (bf16[4,4,48,512]{3,2,1,0:T(8,128)(2,1)}, bf16[4,4,48,512]{3,2,1,0:T(8,128)(2,1)S(1)}, u32[]{:S(2)}, u32[]{:S(2)}) collective-permute-start(bf16[4,4,48,512]{3,2,1,0:T(8,128)(2,1)} %get-tuple-element.239), channel_id=1, source_target_pairs={{0,1},{1,0},{2,3},{3,2},{4,5},{5,4},{6,7},{7,6},{8,9},{9,8},{10,11... | collective-permute-start | bytes 2359304 | tf_op jit(solution)/shard_map/ppermute | solution.py:1060
  281.8 12.3 %collective-permute-start.19 = (bf16[4,112,512]{2,1,0:T(8,128)(2,1)}, bf16[4,112,512]{2,1,0:T(8,128)(2,1)S(1)}, u32[]{:S(2)}, u32[]{:S(2)}) collective-permute-start(bf16[4,112,512]{2,1,0:T(8,128)(2,1)} %get-tuple-element.236), channel_id=1, source_target_pairs={{0,16},{8,24},{16,0},{24,8},{1,17},{9,25},{17,1},{25,9},{2,18},{10... | collective-permute-start | bytes 1376264 | tf_op jit(solution)/shard_map/ppermute | solution.py:1060
  283.4 12.0 %collective-permute-start.20 = (bf16[4,112,512]{2,1,0:T(8,128)(2,1)}, bf16[4,112,512]{2,1,0:T(8,128)(2,1)S(1)}, u32[]{:S(2)}, u32[]{:S(2)}) collective-permute-start(bf16[4,112,512]{2,1,0:T(8,128)(2,1)} %get-tuple-element.237), channel_id=1, source_target_pairs={{0,8},{8,0},{16,24},{24,16},{1,9},{9,1},{17,25},{25,17},{2,10},{10... | collective-permute-start | bytes 1376264 | tf_op jit(solution)/shard_map/ppermute | solution.py:1060
  287.2 20.0 %copy-start.28 = (bf16[192,512]{1,0:T(8,128)(2,1)S(1)}, bf16[192,512]{1,0:T(8,128)(2,1)}, u32[]{:S(2)}) copy-start(bf16[192,512]{1,0:T(8,128)(2,1)} %get-tuple-element.259) | copy-start | bytes 589828
  299.8 7.4 %collective-permute-start.24 = (bf16[128,512]{1,0:T(8,128)(2,1)S(1)}, bf16[128,512]{1,0:T(8,128)(2,1)S(1)}, u32[]{:S(2)}, u32[]{:S(2)}) collective-permute-start(bf16[128,512]{1,0:T(8,128)(2,1)S(1)} %bitcast.135), channel_id=1, source_target_pairs={{0,24},{8,16},{16,8},{24,0},{1,25},{9,17},{17,9},{25,1},{2,26},{10... | collective-permute-start | bytes 393224 | tf_op jit(solution)/shard_map/ppermute | solution.py:1060
  300.2 24.7 %collective-permute-start.23 = (bf16[128,512]{1,0:T(8,128)(2,1)S(1)}, bf16[128,512]{1,0:T(8,128)(2,1)S(1)}, u32[]{:S(2)}, u32[]{:S(2)}) collective-permute-start(bf16[128,512]{1,0:T(8,128)(2,1)S(1)} %bitcast.136), channel_id=1, source_target_pairs={{0,16},{8,24},{16,0},{24,8},{1,17},{9,25},{17,1},{25,9},{2,18},{10... | collective-permute-start | bytes 393224 | tf_op jit(solution)/shard_map/ppermute | solution.py:1060
  301.8 23.1 %collective-permute-start.22 = (bf16[128,512]{1,0:T(8,128)(2,1)S(1)}, bf16[128,512]{1,0:T(8,128)(2,1)S(1)}, u32[]{:S(2)}, u32[]{:S(2)}) collective-permute-start(bf16[128,512]{1,0:T(8,128)(2,1)S(1)} %bitcast.137), channel_id=1, source_target_pairs={{0,8},{8,0},{16,24},{24,16},{1,9},{9,1},{17,25},{25,17},{2,10},{10... | collective-permute-start | bytes 393224 | tf_op jit(solution)/shard_map/ppermute | solution.py:1060
  303.3 23.2 %collective-permute-start.25 = (bf16[192,512]{1,0:T(8,128)(2,1)}, bf16[192,512]{1,0:T(8,128)(2,1)S(1)}, u32[]{:S(2)}, u32[]{:S(2)}) collective-permute-start(bf16[192,512]{1,0:T(8,128)(2,1)} %get-tuple-element.257), channel_id=1, source_target_pairs={{0,8},{8,0},{16,24},{24,16},{1,9},{9,1},{17,25},{25,17},{2,10},{10... | collective-permute-start | bytes 589832 | tf_op jit(solution)/shard_map/ppermute | solution.py:1060
  303.9 22.6 %collective-permute-start.26 = (bf16[192,512]{1,0:T(8,128)(2,1)S(1)}, bf16[192,512]{1,0:T(8,128)(2,1)S(1)}, u32[]{:S(2)}, u32[]{:S(2)}) collective-permute-start(bf16[192,512]{1,0:T(8,128)(2,1)S(1)} %copy-done.29), channel_id=1, source_target_pairs={{0,16},{8,24},{16,0},{24,8},{1,17},{9,25},{17,1},{25,9},{2,18},{10... | collective-permute-start | bytes 589832 | tf_op jit(solution)/shard_map/ppermute | solution.py:1060
  307.2 19.3 %collective-permute-start.27 = (bf16[192,512]{1,0:T(8,128)(2,1)S(1)}, bf16[192,512]{1,0:T(8,128)(2,1)S(1)}, u32[]{:S(2)}, u32[]{:S(2)}) collective-permute-start(bf16[192,512]{1,0:T(8,128)(2,1)S(1)} %copy-done.28), channel_id=1, source_target_pairs={{0,24},{8,16},{16,8},{24,0},{1,25},{9,17},{17,9},{25,1},{2,26},{10... | collective-permute-start | bytes 589832 | tf_op jit(solution)/shard_map/ppermute | solution.py:1060
  307.5 44.1 %copy-start.3 = (bf16[4,14,14,512]{3,2,1,0:T(8,128)(2,1)S(1)}, bf16[4,14,14,512]{3,2,1,0:T(8,128)(2,1)}, u32[]{:S(2)}) copy-start(bf16[4,14,14,512]{3,2,1,0:T(8,128)(2,1)} %get-tuple-element.302) | copy-start | bytes 2408452
  324.9 28.3 %copy-start = (f32[4,14,14,512]{3,2,1,0:T(8,128)S(1)}, f32[4,14,14,512]{3,2,1,0:T(8,128)}, u32[]{:S(2)}) copy-start(f32[4,14,14,512]{3,2,1,0:T(8,128)} %get-tuple-element.304) | copy-start | bytes 4816900
  325.0 30.5 %copy-start.18 = (bf16[128,512]{1,0:T(8,128)(2,1)}, bf16[128,512]{1,0:T(8,128)(2,1)S(1)}, u32[]{:S(2)}) copy-start(bf16[128,512]{1,0:T(8,128)(2,1)S(1)} %collective-permute-done.23.refs_2_) | copy-start | bytes 393220
  325.0 30.5 %copy-start.19 = (bf16[128,512]{1,0:T(8,128)(2,1)}, bf16[128,512]{1,0:T(8,128)(2,1)S(1)}, u32[]{:S(2)}) copy-start(bf16[128,512]{1,0:T(8,128)(2,1)S(1)} %collective-permute-done.22.refs_1_) | copy-start | bytes 393220
  325.0 1.5 collective-permute-start.28
  329.2 7.0 %collective-permute-start.32 = (bf16[64,512]{1,0:T(8,128)(2,1)}, bf16[64,512]{1,0:T(8,128)(2,1)S(1)}, u32[]{:S(2)}, u32[]{:S(2)}) collective-permute-start(bf16[64,512]{1,0:T(8,128)(2,1)} %get-tuple-element.263), channel_id=1, source_target_pairs={{0,2},{2,0},{4,6},{6,4},{1,3},{3,1},{5,7},{7,5},{8,10},{10,8},{12,... | collective-permute-start | bytes 196616 | tf_op jit(solution)/shard_map/ppermute | solution.py:1060
  329.4 26.0 %collective-permute-start.31 = (bf16[224,512]{1,0:T(8,128)(2,1)}, bf16[224,512]{1,0:T(8,128)(2,1)S(1)}, u32[]{:S(2)}, u32[]{:S(2)}) collective-permute-start(bf16[224,512]{1,0:T(8,128)(2,1)} %bitcast.126), channel_id=1, source_target_pairs={{0,24},{8,16},{16,8},{24,0},{1,25},{9,17},{17,9},{25,1},{2,26},{10... | collective-permute-start | bytes 688136 | tf_op jit(solution)/shard_map/ppermute | solution.py:1060
  332.1 23.4 %collective-permute-start.30 = (bf16[224,512]{1,0:T(8,128)(2,1)}, bf16[224,512]{1,0:T(8,128)(2,1)S(1)}, u32[]{:S(2)}, u32[]{:S(2)}) collective-permute-start(bf16[224,512]{1,0:T(8,128)(2,1)} %bitcast.127), channel_id=1, source_target_pairs={{0,16},{8,24},{16,0},{24,8},{1,17},{9,25},{17,1},{25,9},{2,18},{10... | collective-permute-start | bytes 688136 | tf_op jit(solution)/shard_map/ppermute | solution.py:1060
  332.5 23.0 %collective-permute-start.29 = (bf16[224,512]{1,0:T(8,128)(2,1)}, bf16[224,512]{1,0:T(8,128)(2,1)S(1)}, u32[]{:S(2)}, u32[]{:S(2)}) collective-permute-start(bf16[224,512]{1,0:T(8,128)(2,1)} %bitcast.128), channel_id=1, source_target_pairs={{0,8},{8,0},{16,24},{24,16},{1,9},{9,1},{17,25},{25,17},{2,10},{10... | collective-permute-start | bytes 688136 | tf_op jit(solution)/shard_map/ppermute | solution.py:1060
  332.9 7.6 %collective-permute-start.33 = (bf16[64,512]{1,0:T(8,128)(2,1)}, bf16[64,512]{1,0:T(8,128)(2,1)S(1)}, u32[]{:S(2)}, u32[]{:S(2)}) collective-permute-start(bf16[64,512]{1,0:T(8,128)(2,1)} %get-tuple-element.264), channel_id=1, source_target_pairs={{0,4},{2,6},{4,0},{6,2},{1,5},{3,7},{5,1},{7,3},{8,12},{10,14},{12... | collective-permute-start | bytes 196616 | tf_op jit(solution)/shard_map/ppermute | solution.py:1060
  336.2 6.3 %collective-permute-start.34 = (bf16[64,512]{1,0:T(8,128)(2,1)}, bf16[64,512]{1,0:T(8,128)(2,1)S(1)}, u32[]{:S(2)}, u32[]{:S(2)}) collective-permute-start(bf16[64,512]{1,0:T(8,128)(2,1)} %get-tuple-element.265), channel_id=1, source_target_pairs={{0,6},{2,4},{4,2},{6,0},{1,7},{3,5},{5,3},{7,1},{8,14},{10,12},{12... | collective-permute-start | bytes 196616 | tf_op jit(solution)/shard_map/ppermute | solution.py:1060
  344.7 5.4 %collective-permute-start.37 = (bf16[64,512]{1,0:T(8,128)(2,1)}, bf16[64,512]{1,0:T(8,128)(2,1)S(1)}, u32[]{:S(2)}, u32[]{:S(2)}) collective-permute-start(bf16[64,512]{1,0:T(8,128)(2,1)} %c_sum_line.1.refs_8_), channel_id=1, source_target_pairs={{0,24},{8,16},{16,8},{24,0},{1,25},{9,17},{17,9},{25,1},{2,26},{10... | collective-permute-start | bytes 196616 | tf_op jit(solution)/shard_map/ppermute | solution.py:1060
  347.2 8.2 %collective-permute-start.36 = (bf16[64,512]{1,0:T(8,128)(2,1)}, bf16[64,512]{1,0:T(8,128)(2,1)S(1)}, u32[]{:S(2)}, u32[]{:S(2)}) collective-permute-start(bf16[64,512]{1,0:T(8,128)(2,1)} %c_sum_line.1.refs_8_), channel_id=1, source_target_pairs={{0,16},{8,24},{16,0},{24,8},{1,17},{9,25},{17,1},{25,9},{2,18},{10... | collective-permute-start | bytes 196616 | tf_op jit(solution)/shard_map/ppermute | solution.py:1060
  350.1 5.3 %collective-permute-start.35 = (bf16[64,512]{1,0:T(8,128)(2,1)}, bf16[64,512]{1,0:T(8,128)(2,1)S(1)}, u32[]{:S(2)}, u32[]{:S(2)}) collective-permute-start(bf16[64,512]{1,0:T(8,128)(2,1)} %c_sum_line.1.refs_8_), channel_id=1, source_target_pairs={{0,8},{8,0},{16,24},{24,16},{1,9},{9,1},{17,25},{25,17},{2,10},{10... | collective-permute-start | bytes 196616 | tf_op jit(solution)/shard_map/ppermute | solution.py:1060
  (24 other events, 95.4 us)
Sparse Core Ops, SparseCore 0:
  171.5 12.3 reduce-scatter.6
  193.1 35.7 reduce-scatter.12
  240.8 22.1 reduce-scatter.8
  299.9 23.6 reduce-scatter.10
